TPU v7x, 128 devices: a whole 4x4x4 slice. The times are simulated.
128 devices in a mesh: dp: 16 (over x, y_hi, core), tensor: 8 (over y_lo, z).
Axes of the slice: x: 4, y: 4 (y_hi: 2, y_lo: 2; y = y_hi * 2 + y_lo), z: 4, core: 2. Of those that a mesh axis runs over, the one named last changes fastest.
Arguments:
- grad_values: bfloat16 [2048, 16384], P('tensor', 'dp'), may hold values from -448 to 448
- row_scale: float32 [2048], P('tensor'), may hold values from 0.0004 to 0.004
- gate_input: bfloat16 [2048, 26624], P('dp', 'tensor'), may hold values from -8 to 8
- up_input: bfloat16 [2048, 26624], P('dp', 'tensor'), may hold values from -6 to 6
- down_weight: bfloat16 [26624, 16384], P('tensor', 'dp'), may hold values from -0.0390625 to 0.0390625
Outputs:
- down_grad: float32 [26624, 16384], P('tensor', 'dp')
- gate_grad: bfloat16 [2048, 26624], P('dp', 'tensor')
- up_grad: bfloat16 [2048, 26624], P('dp', 'tensor')
All inputs are finite; a program needn't handle non-finite values.
Results may differ from a plain program's by a relative error of at most 0.039.
Values may be sent and summed in bfloat16 or wider, within the bound.
A program may use at most 128 MiB of HBM per device.

v0:
```python
import jax
import jax.numpy as jnp
from jax import lax
from jax.sharding import PartitionSpec as P


def body(grad_values, row_scale, gate_input, up_input, down_weight):
    values_all, scales_all = (
        lax.all_gather(grad_values, "tensor", axis=0, tiled=True),
        lax.all_gather(row_scale.astype(jnp.bfloat16), "tensor", axis=0, tiled=True).astype(
            row_scale.dtype
        ),
    )
    grad_out = (values_all.astype(jnp.float32) * scales_all[:, None]).astype(jnp.bfloat16)
    gate_float = gate_input.astype(jnp.float32)
    up_float = up_input.astype(jnp.float32)
    sigmoid_gate = jax.nn.sigmoid(gate_float)
    activated = gate_float * sigmoid_gate
    hidden = (activated * up_float).astype(jnp.bfloat16)
    hidden_all = lax.all_gather(hidden, "dp", axis=0, tiled=True)
    down_grad = lax.dot_general(
        hidden_all, grad_out, (((0,), (0,)), ((), ())), preferred_element_type=jnp.float32
    )
    partial_grad = lax.dot_general(
        grad_out, down_weight, (((1,), (1,)), ((), ())), preferred_element_type=jnp.float32
    )
    hidden_grad = lax.psum_scatter(
        partial_grad.astype(jnp.bfloat16), "dp", scatter_dimension=0, tiled=True
    ).astype(jnp.float32)
    gate_grad = (
        hidden_grad * up_float * sigmoid_gate * (1.0 + gate_float * (1.0 - sigmoid_gate))
    ).astype(jnp.bfloat16)
    up_grad = (hidden_grad * activated).astype(jnp.bfloat16)
    return (down_grad, gate_grad, up_grad)


def solution(mesh):
    return jax.shard_map(
        body,
        mesh=mesh,
        in_specs=(
            P("tensor", "dp"),
            P("tensor"),
            P("dp", "tensor"),
            P("dp", "tensor"),
            P("tensor", "dp"),
        ),
        out_specs=(P("tensor", "dp"), P("dp", "tensor"), P("dp", "tensor")),
        check_vma=False,
    )
```

profile of v0, /device:TPU:1, one launch (start us, length us, event | category | flops | bytes accessed | tf_op | source)
XLA Modules:
  0.0 338.4 jit_solution(18196262237105291989)
XLA Ops:
  7.2 0.0 all-gather.6.cloned.1.call-start
  7.2 0.7 all-gather.6.cloned.1.call-update
  7.9 0.0 reduce-scatter.2.cloned.1.call-start
  7.9 0.7 convert_element_type.37
  8.6 17.2 %all-gather = bf16[8,1,256]{2,1,0:T(2,128)(2,1)S(1)} all-gather(bf16[1,1,256]{2,1,0:T(2,128)(2,1)S(1)} %reshape.7), channel_id=1, replica_groups=mesh['dp'=16,'tensor'=8] {'tensor'}, dimensions={0}, use_global_device_ids=true | all-gather | bytes 4608 | tf_op jit(solution)/shard_map/all_gather | solution.py:10
  25.8 39.9 %all-gather.6.cloned.1.call-done = bf16[2048,1024]{1,0:T(8,128)(2,1)} async-done(((bf16[256,1024]{1,0:T(8,128)(2,1)}), bf16[2048,1024]{1,0:T(8,128)(2,1)}) %all-gather.6.cloned.1.call-update) | async-done | bytes 4194320 | tf_op jit(solution)/shard_map/all_gather | solution.py:9
  65.7 21.0 %convolution_convert_fusion = bf16[2048,3328]{1,0:T(8,128)(2,1)} fusion(bf16[3328,1024]{1,0:T(8,128)(2,1)} %param.9, bf16[2048,1024]{1,0:T(8,128)(2,1)} %all-gather.6.cloned.1.call-done, f32[2048]{0:T(1024)S(1)} %bitcast.3), kind=kOutput, calls=%fused_computation | convolution fusion | flops 13971750912 | bytes 24649728 | tf_op jit(solution)/shard_map/dot_general | solution.py:24
  86.7 0.0 copy-start
  86.7 0.0 copy-start.1
  86.7 0.0 reduce-scatter.2.cloned.1.call-update
  86.7 0.2 all-gather.4.cloned.1.call-start
  87.0 124.7 %reduce-scatter.2.cloned.1.call-done = bf16[128,3328]{1,0:T(8,128)(2,1)} async-done(((bf16[2048,3328]{1,0:T(8,128)(2,1)}), bf16[128,3328]{1,0:T(8,128)(2,1)}) %reduce-scatter.2.cloned.1.call-update) | async-done | bytes 851984 | tf_op jit(solution)/shard_map/reduce_scatter | solution.py:27
  211.6 0.0 copy-done
  211.6 0.0 copy-done.1
  211.6 3.5 %fusion.5 = (bf16[128,3328]{1,0:T(8,128)(2,1)}, bf16[128,3328]{1,0:T(8,128)(2,1)}, bf16[128,3328]{1,0:T(8,128)(2,1)}) fusion(bf16[128,3328]{1,0:T(8,128)(2,1)} %reduce-scatter.2.cloned.1.call-done, bf16[128,3328]{1,0:T(8,128)(2,1)S(1)} %copy-done, bf16[128,3328]{1,0:T(8,128)(2,1)S(1)} %copy-done.1), kind=kLoop, calls=%fused_computation.13 | loop fusion | flops 7667712 | bytes 5111808 | tf_op jit(solution)/shard_map/convert_element_type | solution.py:33
  215.2 0.0 all-gather.4.cloned.1.call-update
  215.2 95.2 %all-gather.4.cloned.1.call-done = bf16[2048,3328]{1,0:T(8,128)(2,1)} async-done(((bf16[128,3328]{1,0:T(8,128)(2,1)}), bf16[2048,3328]{1,0:T(8,128)(2,1)}) %all-gather.4.cloned.1.call-update) | async-done | bytes 13631504 | tf_op jit(solution)/shard_map/all_gather | solution.py:20
  310.4 21.5 %fusion = f32[3328,1024]{1,0:T(8,128)} fusion(bf16[2048,3328]{1,0:T(8,128)(2,1)} %all-gather.4.cloned.1.call-done, bf16[2048,1024]{1,0:T(8,128)(2,1)} %all-gather.6.cloned.1.call-done, f32[2048]{0:T(1024)S(1)} %bitcast.4), kind=kOutput, calls=%fused_computation.8 | convolution fusion | flops 13964935168 | bytes 31465472 | tf_op jit(solution)/shard_map/dot_general | solution.py:21
  (2 shorter events, 0.0 us)
Async XLA Ops:
  7.2 58.6 %all-gather.6.cloned.1.call-start = ((), (), s32[]{:S(2)}) async-start(), calls=%async_computation.2 | async-start | bytes 4718592 | tf_op jit(solution)/shard_map/all_gather | solution.py:9
  7.9 203.7 %reduce-scatter.2.cloned.1.call-start = ((), (), s32[]{:S(2)}) async-start(), calls=%async_computation.3 | async-start | bytes 14483456 | tf_op jit(solution)/shard_map/reduce_scatter | solution.py:27
  86.7 124.9 %copy-start = (bf16[128,3328]{1,0:T(8,128)(2,1)S(1)}, bf16[128,3328]{1,0:T(8,128)(2,1)}, u32[]{:S(2)}) copy-start(bf16[128,3328]{1,0:T(8,128)(2,1)} %param.7) | copy-start | bytes 2555908
  86.7 124.9 %copy-start.1 = (bf16[128,3328]{1,0:T(8,128)(2,1)S(1)}, bf16[128,3328]{1,0:T(8,128)(2,1)}, u32[]{:S(2)}) copy-start(bf16[128,3328]{1,0:T(8,128)(2,1)} %param.8) | copy-start | bytes 2555908
  86.7 223.7 %all-gather.4.cloned.1.call-start = ((), (), s32[]{:S(2)}) async-start(), calls=%async_computation.1 | async-start | bytes 14483456 | tf_op jit(solution)/shard_map/all_gather | solution.py:20
Sparse Core Ops, SparseCore 0:
  9.6 56.0 all-gather.5
  86.9 124.7 reduce-scatter.1
  215.3 95.0 all-gather.3
where the time goes:
time: 339 us; the launch traced here: 338 us
  waiting for transfers between devices  260 us (77%)
  matrix products  42.5 us (13%)
  blocking collectives  17.2 us (5%)
  between operations  13.8 us (4%)
  other arithmetic  4.21 us (1%)
    reduce_scatter x1, waiting for transfers between devices, body(): lax.psum_scatter(partial_grad.astype(jnp.bfloat16), 'dp', scatter_dimensi...  125 us
    all_gather x1, waiting for transfers between devices, body(): hidden_all = lax.all_gather(hidden, 'dp', axis=0, tiled=True)  95.2 us
    all_gather x1, waiting for transfers between devices, body(): lax.all_gather(grad_values, 'tensor', axis=0, tiled=True)  39.9 us
    dot_general x1, matrix products, body(): lax.dot_general(hidden_all, grad_out, (((0,), (0,)), ((), ())), preferred...  21.5 us
    dot_general x1, matrix products, body(): lax.dot_general(grad_out, down_weight, (((1,), (1,)), ((), ())), preferre...  21 us
    all_gather x1, blocking collectives, body(): lax.all_gather(row_scale.astype(jnp.bfloat16), 'tensor', axis=0, tiled=True)  17.2 us
  transfers between devices with their start and end apart: 3, of which 3 were waited for; matrix products, arithmetic and copies ran while one was open for 0% of the time, Pallas kernels for 0%

commit v1 on v0

v1 whole, which is shorter than its diff:
```python
import functools

import jax
import jax.numpy as jnp
from jax import lax
from jax.experimental import pallas as pl
from jax.experimental.pallas import tpu as pltpu
from jax.sharding import PartitionSpec as P

MESH = pl.DeviceIdType.MESH
BF16 = jnp.bfloat16
F32 = jnp.float32

TOK = 2048
FFL = 3328
HALF = FFL // 2
DL = 1024
N1 = 1024
N2 = HALF - N1
N_COPIES = 96


class Copies:
    def __init__(self, send_sem, recv_sem):
        self.send_sem, self.recv_sem = send_sem, recv_sem
        self.sent = []

    def send(self, src, dst, device):
        index = len(self.sent)
        copy = pltpu.make_async_remote_copy(
            src_ref=src,
            dst_ref=dst,
            send_sem=self.send_sem.at[index],
            recv_sem=self.recv_sem.at[index],
            device_id=device,
            device_id_type=MESH,
        )
        copy.start()
        self.sent.append(copy)
        return index

    def arrived(self, index):
        self.sent[index].wait_recv()

    def finish(self):
        for copy in self.sent:
            copy.wait_send()


def kernel(
    values, scale, gate, up, weight,
    dg_out, gg_out, ug_out,
    g_all, w_both, h_all, p1, p2, r1a, r1b, r1y, r2y, r2a, r2b,
    hg, fin, v_in, gate_in, up_in, dg_buf,
    send_sem, recv_sem, load_sem, dg_sem,
):
    dp = lax.axis_index("dp")
    tensor = lax.axis_index("tensor")
    c = lax.rem(dp, 2)
    yh = lax.rem(dp // 2, 2)
    x = dp // 4
    yl = tensor // 4
    z = lax.rem(tensor, 4)
    q = dp // 2

    def wrap(i):
        return lax.rem(i + 4, 4)

    xr, xl, xf = wrap(x + 1), wrap(x - 1), wrap(x + 2)
    zr, zl, zf = wrap(z + 1), wrap(z - 1), wrap(z + 2)
    to_xr = (xr * 4 + yh * 2 + c, tensor)
    to_xl = (xl * 4 + yh * 2 + c, tensor)
    to_yh = (x * 4 + (1 - yh) * 2 + c, tensor)
    to_core = (q * 2 + (1 - c), tensor)
    to_yl = (dp, (1 - yl) * 4 + z)
    to_zr = (dp, yl * 4 + zr)
    to_zl = (dp, yl * 4 + zl)

    def chip(xx, yy):
        return xx * 2 + yy

    def load(i, src, dst):
        copy = pltpu.make_async_copy(src, dst, load_sem.at[i])
        copy.start()
        return copy

    own_half = pl.ds(pl.multiple_of(c * HALF, 128), HALF)
    sib_half = pl.ds(pl.multiple_of((1 - c) * HALF, 128), HALF)
    load_v = load(0, values, v_in)
    load_g = load(1, gate, gate_in)
    load_u = load(2, up, up_in)
    load_w = load(3, weight.at[own_half], w_both.at[c])

    barrier = pltpu.get_barrier_semaphore()
    for neighbour in (to_xr, to_xl, to_yh, to_core, to_yl, to_zr, to_zl):
        pl.semaphore_signal(barrier, inc=1, device_id=neighbour, device_id_type=MESH)
    pl.semaphore_wait(barrier, 7)

    net = Copies(send_sem, recv_sem)
    send, arrived = net.send, net.arrived

    def g_rows(block, first=0, rows=256):
        return g_all.at[c, pl.ds(pl.multiple_of(block * 256 + first, 128), rows)]

    def send_g(block, device, first=0, rows=256):
        ref = g_rows(block, first, rows)
        return send(ref, ref, device)

    load_v.wait()
    own = tensor
    for i in range(2):
        col = jnp.broadcast_to(scale[i : i + 1, :], (128, 128)).T
        for k in range(DL // 128):
            part = v_in[i * 128 : (i + 1) * 128, k * 128 : (k + 1) * 128].astype(F32) * col
            g_all[c, pl.ds(pl.multiple_of(own * 256 + i * 128, 128), 128), k * 128 : (k + 1) * 128] = part.astype(BF16)
    a_yl = send_g(own, to_yl)
    a_zr = send_g(own, to_zr)
    a_zl = send_g(own, to_zl)
    s_own = send_g(own, to_core)
    w_sib = send(weight.at[sib_half], w_both.at[c], to_core)

    load_g.wait()
    load_u.wait()

    def hidden_tile(k, _):
        cols = pl.ds(pl.multiple_of(k * 128, 128), 128)
        gate_f = gate_in[:, cols].astype(F32)
        h = gate_f * jax.nn.sigmoid(gate_f) * up_in[:, cols].astype(F32)
        h_all[dp, cols, :] = h.T.astype(BF16)
        return 0

    lax.fori_loop(0, FFL // 128, hidden_tile, 0, unroll=2)

    base = pl.multiple_of(c * HALF, 128)
    rows1 = pl.ds(base, N1)
    rows2 = pl.ds(pl.multiple_of(base + N1, 128), N2)

    def send_h(first, count, rows, device):
        ref = h_all.at[pl.ds(first, count), rows]
        return send(ref, ref, device)

    both = pl.ds(dp, 1)
    s_h = send(h_all.at[both], h_all.at[both], to_core)
    arrived(s_h)
    b1_y = send_h(2 * q, 2, rows1, to_yh)
    b2_xr = send_h(2 * q, 2, rows2, to_xr)
    b2_xl = send_h(2 * q, 2, rows2, to_xl)
    b1_xr = send_h(2 * q, 2, rows1, to_xr)
    b1_xl = send_h(2 * q, 2, rows1, to_xl)

    sib = []

    def share_h(first, count, rows):
        sib.append(send_h(first, count, rows, to_core))

    def product(block):
        rows = pl.ds(pl.multiple_of(block * 256, 256), 256)

        def cols_of(first, width):
            w_rows = pl.ds(first, width)
            total = lax.dot_general(
                g_all[0, rows, :], w_both[0, w_rows, :], (((1,), (1,)), ((), ())), preferred_element_type=F32
            )
            total += lax.dot_general(
                g_all[1, rows, :], w_both[1, w_rows, :], (((1,), (1,)), ((), ())), preferred_element_type=F32
            )
            return total.astype(BF16)

        def tile(n, _):
            first = pl.multiple_of(n * 256, 256)
            p1[block, :, pl.ds(first, 256)] = cols_of(first, 256)
            return 0

        lax.fori_loop(0, N1 // 256, tile, 0)
        p2[block, :, :] = cols_of(N1, N2)

    other = (1 - yl) * 4 + z
    arrived(a_yl)
    a_yzr = send_g(other, to_zr)
    a_yzl = send_g(other, to_zl)
    s_other = send_g(other, to_core)

    qy = chip(x, 1 - yh)
    arrived(b1_y)
    b1_yxr = send_h(2 * qy, 2, rows1, to_xr)
    b1_yxl = send_h(2 * qy, 2, rows1, to_xl)
    b2_y = send_h(2 * q, 2, rows2, to_yh)
    share_h(2 * qy, 2, rows1)

    arrived(a_zr)
    a_fr = send_g(yl * 4 + zl, to_zr, 0, 128)
    s_zl = send_g(yl * 4 + zl, to_core)
    arrived(a_zl)
    a_fl = send_g(yl * 4 + zr, to_zl, 128, 128)
    s_zr = send_g(yl * 4 + zr, to_core)

    ql, qr, qf = chip(xl, yh), chip(xr, yh), chip(xf, yh)
    arrived(b2_xr)
    b2_fr = send_h(2 * ql, 1, rows2, to_xr)
    b2_yl = send_h(2 * ql, 2, rows2, to_yh)
    share_h(2 * ql, 2, rows2)
    arrived(b2_xl)
    b2_fl = send_h(2 * qr + 1, 1, rows2, to_xl)
    b2_yr = send_h(2 * qr, 2, rows2, to_yh)
    share_h(2 * qr, 2, rows2)

    arrived(b1_xr)
    b1_fr = send_h(2 * ql, 1, rows1, to_xr)
    share_h(2 * ql, 2, rows1)
    arrived(b1_xl)
    b1_fl = send_h(2 * qr + 1, 1, rows1, to_xl)
    share_h(2 * qr, 2, rows1)

    load_w.wait()
    arrived(w_sib)
    arrived(s_own)
    arrived(s_other)

    def near(i, _):
        product(i * 4 + z)
        return 0

    lax.fori_loop(0, 2, near, 0)

    ol = (1 - yl) * 4 + zl
    orr = (1 - yl) * 4 + zr
    arrived(a_yzr)
    a_yfr = send_g(ol, to_zr, 0, 128)
    s_ol = send_g(ol, to_core)
    arrived(a_yzl)
    a_yfl = send_g(orr, to_zl, 128, 128)
    s_or = send_g(orr, to_core)

    arrived(b2_fr)
    arrived(b2_fl)
    b2_yf = send_h(2 * qf, 2, rows2, to_yh)
    share_h(2 * qf, 2, rows2)

    qyl, qyr, qyf = chip(xl, 1 - yh), chip(xr, 1 - yh), chip(xf, 1 - yh)
    arrived(b1_yxr)
    b1_yfr = send_h(2 * qyl, 1, rows1, to_xr)
    share_h(2 * qyl, 2, rows1)
    arrived(b1_yxl)
    b1_yfl = send_h(2 * qyr + 1, 1, rows1, to_xl)
    share_h(2 * qyr, 2, rows1)

    arrived(a_fr)
    arrived(a_fl)
    s_f = send_g(yl * 4 + zf, to_core)

    for s in (s_zl, s_zr, s_ol, s_or):
        arrived(s)

    def middle(i, _):
        product((i // 2) * 4 + wrap(z - 1 + 2 * lax.rem(i, 2)))
        return 0

    lax.fori_loop(0, 4, middle, 0)

    arrived(a_yfr)
    arrived(a_yfl)
    s_of = send_g((1 - yl) * 4 + zf, to_core)
    arrived(s_f)
    arrived(s_of)

    def far(i, _):
        product(i * 4 + zf)
        return 0

    lax.fori_loop(0, 2, far, 0)

    top, low = pl.ds(0, 128), pl.ds(128, 128)
    lows, tops = [], []
    for yy in range(2):
        bf = chip(xf, yy)
        lows.append(send(p1.at[bf, top], r1a.at[0, yy], to_xr))
        tops.append(send(p1.at[bf, low], r1a.at[1, yy], to_xl))
    c2y_f = send(p2.at[chip(xf, 1 - yh)], r2y.at[xf], to_yh)
    c2y_r = send(p2.at[chip(xr, 1 - yh)], r2y.at[xr], to_yh)
    c2y_l = send(p2.at[chip(xl, 1 - yh)], r2y.at[xl], to_yh)
    c2y_o = send(p2.at[chip(x, 1 - yh)], r2y.at[x], to_yh)
    c1 = [[], []]
    for yy in range(2):
        c1[yy].append(send(p1.at[chip(xr, yy), low], r1b.at[0, yy, low], to_xr))
        c1[yy].append(send(p1.at[chip(xl, yy), top], r1b.at[1, yy, top], to_xl))

    arrived(b1_fr)
    arrived(b1_fl)
    share_h(2 * qf, 2, rows1)
    arrived(b2_y)
    share_h(2 * qy, 2, rows2)
    arrived(b2_yl)
    share_h(2 * qyl, 2, rows2)
    arrived(b2_yr)
    share_h(2 * qyr, 2, rows2)

    def add(dst, rows, others):
        def strip(i, _):
            at = pl.ds(pl.multiple_of(rows[0] + i * 16, 16), 16)
            total = dst[at, :].astype(F32)
            for other_ref, shift in others:
                total += other_ref[pl.ds(pl.multiple_of(rows[0] - shift + i * 16, 16), 16), :].astype(F32)
            dst[at, :] = total.astype(BF16)
            return 0

        lax.fori_loop(0, rows[1] // 16, strip, 0)

    for yy in range(2):
        arrived(lows[yy])
        add(p1.at[chip(xr, yy)], (0, 128), [(r1a.at[0, yy], 0)])
        c1[yy].append(send(p1.at[chip(xr, yy), top], r1b.at[0, yy, top], to_xr))
        arrived(tops[yy])
        add(p1.at[chip(xl, yy)], (128, 128), [(r1a.at[1, yy], 128)])
        c1[yy].append(send(p1.at[chip(xl, yy), low], r1b.at[1, yy, low], to_xl))

    arrived(b1_yfr)
    arrived(b1_yfl)
    share_h(2 * qyf, 2, rows1)
    arrived(b2_yf)
    share_h(2 * qyf, 2, rows2)
    for s in sib:
        arrived(s)

    def dg_copy(slot, m):
        return pltpu.make_async_copy(
            dg_buf.at[slot], dg_out.at[pl.ds(pl.multiple_of(m * 128, 128), 128)], dg_sem.at[slot]
        )

    def dg_tile(m, _):
        slot = lax.rem(m, 2)

        @pl.when(m >= 2)
        def _():
            dg_copy(slot, m).wait()

        rows = pl.ds(pl.multiple_of(m * 128, 128), 128)
        lhs = jnp.concatenate([h_all[s, rows, :] for s in range(16)], axis=1)
        dg_buf[slot] = jnp.dot(lhs, g_all[c], preferred_element_type=F32)
        dg_copy(slot, m).start()
        return 0

    def down(first, last):
        lax.fori_loop(first, last, dg_tile, 0)

    down(0, 4)
    arrived(c2y_f)
    bf = chip(xf, yh)
    add(p2.at[bf], (0, 256), [(r2y.at[xf], 0)])
    c2a_r = send(p2.at[bf, top], r2a.at[0], to_xr)
    c2a_l = send(p2.at[bf, low], r2a.at[1], to_xl)
    down(4, 9)
    arrived(c2y_r)
    br, bl = chip(xr, yh), chip(xl, yh)
    add(p2.at[br], (128, 128), [(r2y.at[xr], 0)])
    c2_r = [send(p2.at[br, low], r2b.at[0, low], to_xr)]
    arrived(c2y_l)
    add(p2.at[bl], (0, 128), [(r2y.at[xl], 0)])
    c2_l = [send(p2.at[bl, top], r2b.at[1, top], to_xl)]
    arrived(c2a_r)
    add(p2.at[br], (0, 128), [(r2y.at[xr], 0), (r2a.at[0], 0)])
    c2_r.append(send(p2.at[br, top], r2b.at[0, top], to_xr))
    arrived(c2a_l)
    add(p2.at[bl], (128, 128), [(r2y.at[xl], 0), (r2a.at[1], 128)])
    c2_l.append(send(p2.at[bl, low], r2b.at[1, low], to_xl))
    down(9, 16)

    for s in c1[0] + c1[1]:
        arrived(s)
    bo = chip(x, 1 - yh)
    add(p1.at[bo], (0, 256), [(r1b.at[0, 1 - yh], 0), (r1b.at[1, 1 - yh], 0)])
    c1_y = send(p1.at[bo], r1y, to_yh)
    down(16, 26)

    own_rows = pl.multiple_of(c * 128, 128)
    sib_rows = pl.multiple_of((1 - c) * 128, 128)

    def total_of(first, dst, cols, terms):
        def strip(i, _):
            at = pl.ds(pl.multiple_of(first + i * 16, 16), 16)
            total = terms[0][at, :].astype(F32)
            for term in terms[1:]:
                total += term[at, :].astype(F32)
            dst[pl.ds(pl.multiple_of(i * 16, 16), 16), cols] = total
            return 0

        lax.fori_loop(0, 8, strip, 0)

    for s in c2_r + c2_l + [c2y_o]:
        arrived(s)
    terms2 = [p2.at[q], r2y.at[x], r2b.at[0], r2b.at[1]]
    terms1 = [p1.at[q], r1b.at[0, yh], r1b.at[1, yh], r1y]
    cols1, cols2 = slice(0, N1), slice(N1, HALF)
    total_of(sib_rows, fin, cols2, terms2)
    total_of(own_rows, hg.at[c], cols2, terms2)
    arrived(c1_y)
    total_of(sib_rows, fin, cols1, terms1)
    last = send(fin, hg.at[c], to_core)
    total_of(own_rows, hg.at[c], cols1, terms1)

    def finish_half(half):
        def strip(k, _):
            cols = pl.ds(pl.multiple_of(half * HALF + k * 128, 128), 128)
            grad = hg[half, :, pl.ds(pl.multiple_of(k * 128, 128), 128)]
            gate_f = gate_in[:, cols].astype(F32)
            s = jax.nn.sigmoid(gate_f)
            gg_out[:, cols] = (grad * up_in[:, cols].astype(F32) * s * (1.0 + gate_f * (1.0 - s))).astype(BF16)
            ug_out[:, cols] = (grad * (gate_f * s)).astype(BF16)
            return 0

        lax.fori_loop(0, HALF // 128, strip, 0)

    finish_half(c)
    arrived(last)
    finish_half(1 - c)

    for slot in range(2):
        dg_copy(slot, 24 + slot).wait()
    net.finish()


def body(grad_values, row_scale, gate_input, up_input, down_weight):
    any_spec = pl.BlockSpec(memory_space=pl.ANY)
    vmem_spec = pl.BlockSpec(memory_space=pltpu.VMEM)
    return pl.pallas_call(
        kernel,
        out_shape=(
            jax.ShapeDtypeStruct((FFL, DL), F32),
            jax.ShapeDtypeStruct((128, FFL), BF16),
            jax.ShapeDtypeStruct((128, FFL), BF16),
        ),
        in_specs=[any_spec, vmem_spec, any_spec, any_spec, any_spec],
        out_specs=(any_spec, vmem_spec, vmem_spec),
        scratch_shapes=[
            pltpu.VMEM((2, TOK, DL), BF16),
            pltpu.VMEM((2, HALF, DL), BF16),
            pltpu.VMEM((16, FFL, 128), BF16),
            pltpu.VMEM((8, 256, N1), BF16),
            pltpu.VMEM((8, 256, N2), BF16),
            pltpu.VMEM((2, 2, 128, N1), BF16),
            pltpu.VMEM((2, 2, 256, N1), BF16),
            pltpu.VMEM((256, N1), BF16),
            pltpu.VMEM((4, 256, N2), BF16),
            pltpu.VMEM((2, 128, N2), BF16),
            pltpu.VMEM((2, 256, N2), BF16),
            pltpu.VMEM((2, 128, HALF), F32),
            pltpu.VMEM((128, HALF), F32),
            pltpu.VMEM((256, DL), BF16),
            pltpu.VMEM((128, FFL), BF16),
            pltpu.VMEM((128, FFL), BF16),
            pltpu.VMEM((2, 128, DL), F32),
            pltpu.SemaphoreType.DMA((N_COPIES,)),
            pltpu.SemaphoreType.DMA((N_COPIES,)),
            pltpu.SemaphoreType.DMA((4,)),
            pltpu.SemaphoreType.DMA((2,)),
        ],
        compiler_params=pltpu.CompilerParams(
            collective_id=0, has_side_effects=True, vmem_limit_bytes=62 * 2**20
        ),
        cost_estimate=pl.CostEstimate(flops=4 * TOK * FFL * DL, bytes_accessed=24 * 2**20, transcendentals=2 * 128 * FFL),
    )(grad_values, row_scale.reshape(2, 128), gate_input, up_input, down_weight)


def solution(mesh):
    return jax.shard_map(
        body,
        mesh=mesh,
        in_specs=(
            P("tensor", "dp"),
            P("tensor"),
            P("dp", "tensor"),
            P("dp", "tensor"),
            P("tensor", "dp"),
        ),
        out_specs=(P("tensor", "dp"), P("dp", "tensor"), P("dp", "tensor")),
        check_vma=False,
    )
```

time: 339 us -> 150 us (0.44)
  waiting for transfers between devices: 260 us -> 0 us
  Pallas kernels: 0 us -> 135 us
  matrix products: 42.5 us -> 0 us
  blocking collectives: 17.2 us -> 0 us
  local copies, waits for them, and re-layouts: 0.01 us -> 14.9 us
  between operations: 13.8 us -> 0.66 us
  other arithmetic: 4.21 us -> 0 us
    all_gather x2 -> x0, waiting for transfers between devices: 135 us -> none  [the longest x1 95.2 us: body(): hidden_all = lax.all_gather(hidden, 'dp', axis=0, tiled=True)]
    pallas_call x0 -> x1, Pallas kernels: none -> 135 us  [body(): pl.pallas_call(kernel, out_shape=(jax.ShapeDtypeStruct((FFL, DL), F32), j...]
    reduce_scatter x1 -> x0, waiting for transfers between devices: 125 us -> none  [body(): lax.psum_scatter(partial_grad.astype(jnp.bfloat16), 'dp', scatter_dimensi...]
    dot_general x2 -> x0, matrix products: 42.5 us -> none  [the longest x1 21.5 us: body(): lax.dot_general(hidden_all, grad_out, (((0,), (0,)), ((), ())), preferred...]
    all_gather x1 -> x0, blocking collectives: 17.2 us -> none  [body(): lax.all_gather(row_scale.astype(jnp.bfloat16), 'tensor', axis=0, tiled=True)]
    unnamed x5 -> x7, local copies, waits for them, and re-layouts: 0.01 us -> 14.9 us
    convert_element_type x3 -> x0, other arithmetic: 4.21 us -> none  [the longest x1 3.52 us: body(): up_grad = (hidden_grad * activated).astype(jnp.bfloat16)]
  transfers between devices with their start and end apart: 3 -> 0, of which waited for: 3 -> 0; matrix products, arithmetic and copies ran while one was open for 0% -> 0% of each run, Pallas kernels for 0% -> 0%
where the time goes in v1:
time: 150 us
  Pallas kernels  135 us (90%)
  local copies, waits for them, and re-layouts  14.9 us (10%)
    pallas_call x1, Pallas kernels, body(): pl.pallas_call(kernel, out_shape=(jax.ShapeDtypeStruct((FFL, DL), F32), j...  135 us
    unnamed x7, local copies, waits for them, and re-layouts  14.9 us

profile of v1, /device:TPU:1, one launch (start us, length us, event | category | flops | bytes accessed | tf_op | source)
XLA Modules:
  0.0 150.4 jit_solution(4672011498741201212)
XLA Ops:
  0.6 134.8 %shard_map.76 = (f32[3328,1024]{1,0:T(8,128)}, bf16[128,3328]{1,0:T(8,128)(2,1)}, bf16[128,3328]{1,0:T(8,128)(2,1)}) custom-call(bf16[256,1024]{1,0:T(8,128)(2,1)} %values.1, f32[2,128]{1,0:T(2,128)} %bitcast.1, bf16[128,3328]{1,0:T(8,128)(2,1)} %gate.1, bf16[128,3328]{1,0:T(8,128)(2,1)} %up.1, bf16[3328,1024]{1,0:T(8,128)(2,1)} %weight.1), custom_call_target="tpu_custom_call" | custom-call | flops 27917287424 | bytes 25165824 | tf_op jit(solution)/shard_map/pallas_call | solution.py:424
  135.4 0.0 copy-start.1
  135.4 0.0 copy-start
  135.4 13.1 %copy.11 = f32[3328,1024]{1,0:T(8,128)} copy(f32[3328,1024]{1,0:T(8,128)} %get-tuple-element.6) | data formatting | bytes 27262976
  148.5 0.0 copy-done.1
  148.5 0.9 copy.12
  149.4 0.0 copy-done
  149.5 0.9 copy.13
Async XLA Ops:
  135.4 13.2 %copy-start.1 = (bf16[128,3328]{1,0:T(8,128)(2,1)S(1)}, bf16[128,3328]{1,0:T(8,128)(2,1)}, u32[]{:S(2)}) copy-start(bf16[128,3328]{1,0:T(8,128)(2,1)} %get-tuple-element.7) | copy-start | bytes 2555908
  135.4 14.0 %copy-start = (bf16[128,3328]{1,0:T(8,128)(2,1)S(1)}, bf16[128,3328]{1,0:T(8,128)(2,1)}, u32[]{:S(2)}) copy-start(bf16[128,3328]{1,0:T(8,128)(2,1)} %get-tuple-element.8) | copy-start | bytes 2555908

commit v2 on v1

v2 whole, which is shorter than its diff:
```python
import functools

import jax
import jax.numpy as jnp
from jax import lax
from jax.experimental import pallas as pl
from jax.experimental.pallas import tpu as pltpu
from jax.sharding import PartitionSpec as P

MESH = pl.DeviceIdType.MESH
BF16 = jnp.bfloat16
F32 = jnp.float32

TOK = 2048
FFL = 3328
HALF = FFL // 2
DL = 1024
N1 = 1024
N2 = HALF - N1
N_COPIES = 96


def sigmoid(v):
    return 0.5 * jnp.tanh(0.5 * v) + 0.5


class Copies:
    def __init__(self, send_sem, recv_sem):
        self.send_sem, self.recv_sem = send_sem, recv_sem
        self.sent = []

    def send(self, src, dst, device):
        index = len(self.sent)
        copy = pltpu.make_async_remote_copy(
            src_ref=src,
            dst_ref=dst,
            send_sem=self.send_sem.at[index],
            recv_sem=self.recv_sem.at[index],
            device_id=device,
            device_id_type=MESH,
        )
        copy.start()
        self.sent.append(copy)
        return index

    def arrived(self, index):
        self.sent[index].wait_recv()

    def finish(self):
        for copy in self.sent:
            copy.wait_send()


def kernel(
    values, scale, gate, up, weight,
    dg, hg, gate_in, up_in,
    g_all, w_both, h_all, p1, p2, r1a, r1b, r1y, r2y, r2a, r2b, fin, v_in,
    send_sem, recv_sem, load_sem,
):
    dp = lax.axis_index("dp")
    tensor = lax.axis_index("tensor")
    c = lax.rem(dp, 2)
    yh = lax.rem(dp // 2, 2)
    x = dp // 4
    yl = tensor // 4
    z = lax.rem(tensor, 4)
    q = dp // 2

    def wrap(i):
        return lax.rem(i + 4, 4)

    xr, xl, xf = wrap(x + 1), wrap(x - 1), wrap(x + 2)
    zr, zl, zf = wrap(z + 1), wrap(z - 1), wrap(z + 2)
    to_xr = (xr * 4 + yh * 2 + c, tensor)
    to_xl = (xl * 4 + yh * 2 + c, tensor)
    to_yh = (x * 4 + (1 - yh) * 2 + c, tensor)
    to_core = (q * 2 + (1 - c), tensor)
    to_yl = (dp, (1 - yl) * 4 + z)
    to_zr = (dp, yl * 4 + zr)
    to_zl = (dp, yl * 4 + zl)

    def chip(xx, yy):
        return xx * 2 + yy

    def load(i, src, dst):
        copy = pltpu.make_async_copy(src, dst, load_sem.at[i])
        copy.start()
        return copy

    own_half = pl.ds(pl.multiple_of(c * HALF, 128), HALF)
    sib_half = pl.ds(pl.multiple_of((1 - c) * HALF, 128), HALF)
    load_v = load(0, values, v_in)
    load_g = load(1, gate, gate_in)
    load_u = load(2, up, up_in)

    barrier = pltpu.get_barrier_semaphore()
    for neighbour in (to_xr, to_xl, to_yh, to_core, to_yl, to_zr, to_zl):
        pl.semaphore_signal(barrier, inc=1, device_id=neighbour, device_id_type=MESH)
    pl.semaphore_wait(barrier, 7)

    net = Copies(send_sem, recv_sem)
    send, arrived = net.send, net.arrived

    def g_rows(block, first=0, rows=256):
        return g_all.at[c, pl.ds(pl.multiple_of(block * 256 + first, 128), rows)]

    def send_g(block, device, first=0, rows=256):
        ref = g_rows(block, first, rows)
        return send(ref, ref, device)

    load_v.wait()
    own = tensor
    for i in range(2):
        col = jnp.broadcast_to(scale[i : i + 1, :], (128, 128)).T
        for k in range(DL // 128):
            part = v_in[i * 128 : (i + 1) * 128, k * 128 : (k + 1) * 128].astype(F32) * col
            g_all[c, pl.ds(pl.multiple_of(own * 256 + i * 128, 128), 128), k * 128 : (k + 1) * 128] = part.astype(BF16)
    a_yl = send_g(own, to_yl)
    a_zr = send_g(own, to_zr)
    a_zl = send_g(own, to_zl)
    s_own = send_g(own, to_core)

    load_g.wait()
    load_u.wait()

    def hidden(half):
        def tile(k, _):
            cols = pl.ds(pl.multiple_of(half * HALF + k * 128, 128), 128)
            gate_f = gate_in[:, cols].astype(F32)
            h = gate_f * sigmoid(gate_f) * up_in[:, cols].astype(F32)
            h_all[dp, cols, :] = h.T.astype(BF16)
            return 0

        lax.fori_loop(0, HALF // 128, tile, 0, unroll=True)

    base = pl.multiple_of(c * HALF, 128)
    rows1 = pl.ds(base, N1)
    rows2 = pl.ds(pl.multiple_of(base + N1, 128), N2)

    def send_h(first, count, rows, device):
        ref = h_all.at[pl.ds(first, count), rows]
        return send(ref, ref, device)

    hidden(1 - c)
    s_h = send_h(dp, 1, sib_half, to_core)
    hidden(c)
    arrived(s_h)
    b2_xr = send_h(2 * q, 2, rows2, to_xr)
    b2_xl = send_h(2 * q, 2, rows2, to_xl)
    b1_y = send_h(2 * q, 2, rows1, to_yh)
    b1_xr = send_h(2 * q, 2, rows1, to_xr)
    b1_xl = send_h(2 * q, 2, rows1, to_xl)
    b2_y = send_h(2 * q, 2, rows2, to_yh)
    load_w = load(3, weight.at[own_half], w_both.at[c])
    w_sib = send(weight.at[sib_half], w_both.at[c], to_core)

    sib = [send_h(dp, 1, own_half, to_core)]

    def share_h(first, count, rows):
        sib.append(send_h(first, count, rows, to_core))

    def product(block):
        rows = pl.ds(pl.multiple_of(block * 256, 256), 256)

        def cols_of(first, width):
            w_rows = pl.ds(first, width)
            total = lax.dot_general(
                g_all[0, rows, :], w_both[0, w_rows, :], (((1,), (1,)), ((), ())), preferred_element_type=F32
            )
            total += lax.dot_general(
                g_all[1, rows, :], w_both[1, w_rows, :], (((1,), (1,)), ((), ())), preferred_element_type=F32
            )
            return total.astype(BF16)

        def tile(n, _):
            first = pl.multiple_of(n * 256, 256)
            p1[block, :, pl.ds(first, 256)] = cols_of(first, 256)
            return 0

        lax.fori_loop(0, N1 // 256, tile, 0)
        p2[block, :, :] = cols_of(N1, N2)

    ql, qr, qf = chip(xl, yh), chip(xr, yh), chip(xf, yh)
    qy, qyl, qyr, qyf = chip(x, 1 - yh), chip(xl, 1 - yh), chip(xr, 1 - yh), chip(xf, 1 - yh)
    other = (1 - yl) * 4 + z
    ol, orr = (1 - yl) * 4 + zl, (1 - yl) * 4 + zr

    arrived(b2_xr)
    b2_fr = send_h(2 * ql, 1, rows2, to_xr)
    b2_yl = send_h(2 * ql, 2, rows2, to_yh)
    arrived(b2_xl)
    b2_fl = send_h(2 * qr + 1, 1, rows2, to_xl)
    b2_yr = send_h(2 * qr, 2, rows2, to_yh)

    arrived(a_yl)
    a_yzr = send_g(other, to_zr)
    a_yzl = send_g(other, to_zl)
    s_other = send_g(other, to_core)
    arrived(a_zr)
    a_fr = send_g(yl * 4 + zl, to_zr, 0, 128)
    s_zl = send_g(yl * 4 + zl, to_core)
    arrived(a_zl)
    a_fl = send_g(yl * 4 + zr, to_zl, 128, 128)
    s_zr = send_g(yl * 4 + zr, to_core)
    share_h(2 * ql, 2, rows2)
    share_h(2 * qr, 2, rows2)

    load_w.wait()
    arrived(w_sib)
    arrived(s_own)
    arrived(s_other)

    def near(i, _):
        product(i * 4 + z)
        return 0

    lax.fori_loop(0, 2, near, 0)

    arrived(b1_xr)
    b1_fr = send_h(2 * ql, 1, rows1, to_xr)
    arrived(b1_xl)
    b1_fl = send_h(2 * qr + 1, 1, rows1, to_xl)

    arrived(a_yzr)
    a_yfr = send_g(ol, to_zr, 0, 128)
    s_ol = send_g(ol, to_core)
    arrived(a_yzl)
    a_yfl = send_g(orr, to_zl, 128, 128)
    s_or = send_g(orr, to_core)

    arrived(b1_y)
    b1_yxr = send_h(2 * qy, 2, rows1, to_xr)
    b1_yxl = send_h(2 * qy, 2, rows1, to_xl)
    share_h(2 * ql, 2, rows1)
    share_h(2 * qr, 2, rows1)
    share_h(2 * qy, 2, rows1)

    arrived(b2_fr)
    arrived(b2_fl)
    b2_yf = send_h(2 * qf, 2, rows2, to_yh)
    share_h(2 * qf, 2, rows2)

    for s in (s_zl, s_zr, s_ol, s_or):
        arrived(s)

    def middle(i, _):
        product((i // 2) * 4 + wrap(z - 1 + 2 * lax.rem(i, 2)))
        return 0

    lax.fori_loop(0, 4, middle, 0)

    arrived(a_fr)
    arrived(a_fl)
    s_f = send_g(yl * 4 + zf, to_core)
    arrived(a_yfr)
    arrived(a_yfl)
    s_of = send_g((1 - yl) * 4 + zf, to_core)

    arrived(b1_yxr)
    b1_yfr = send_h(2 * qyl, 1, rows1, to_xr)
    arrived(b1_yxl)
    b1_yfl = send_h(2 * qyr + 1, 1, rows1, to_xl)

    arrived(s_f)
    arrived(s_of)

    def far(i, _):
        product(i * 4 + zf)
        return 0

    lax.fori_loop(0, 2, far, 0)

    top, low = pl.ds(0, 128), pl.ds(128, 128)
    c1 = [[], []]

    def step1(place, yy):
        block = chip(xf, yy)
        return (
            send(p1.at[block, top], r1a.at[0, place], to_xr),
            send(p1.at[block, low], r1a.at[1, place], to_xl),
        )

    def step2_ready(place, yy):
        c1[place].append(send(p1.at[chip(xr, yy), low], r1b.at[0, place, low], to_xr))
        c1[place].append(send(p1.at[chip(xl, yy), top], r1b.at[1, place, top], to_xl))

    def add(dst, rows, others):
        def strip(i, _):
            at = pl.ds(pl.multiple_of(rows[0] + i * 16, 16), 16)
            total = dst[at, :].astype(F32)
            for other_ref, shift in others:
                total += other_ref[pl.ds(pl.multiple_of(rows[0] - shift + i * 16, 16), 16), :].astype(F32)
            dst[at, :] = total.astype(BF16)
            return 0

        lax.fori_loop(0, rows[1] // 16, strip, 0, unroll=2)

    def step2_rest(place, yy, first):
        arrived(first[0])
        add(p1.at[chip(xr, yy)], (0, 128), [(r1a.at[0, place], 0)])
        c1[place].append(send(p1.at[chip(xr, yy), top], r1b.at[0, place, top], to_xr))
        arrived(first[1])
        add(p1.at[chip(xl, yy)], (128, 128), [(r1a.at[1, place], 128)])
        c1[place].append(send(p1.at[chip(xl, yy), low], r1b.at[1, place, low], to_xl))

    first0 = step1(0, 1 - yh)
    c2y_f = send(p2.at[chip(xf, 1 - yh)], r2y.at[xf], to_yh)
    step2_ready(0, 1 - yh)
    c2y_r = send(p2.at[chip(xr, 1 - yh)], r2y.at[xr], to_yh)
    c2y_l = send(p2.at[chip(xl, 1 - yh)], r2y.at[xl], to_yh)
    first1 = step1(1, yh)
    c2y_o = send(p2.at[chip(x, 1 - yh)], r2y.at[x], to_yh)

    arrived(b1_fr)
    arrived(b1_fl)
    share_h(2 * qf, 2, rows1)
    arrived(b2_y)
    share_h(2 * qy, 2, rows2)
    arrived(b2_yl)
    share_h(2 * qyl, 2, rows2)
    arrived(b2_yr)
    share_h(2 * qyr, 2, rows2)
    share_h(2 * qyl, 2, rows1)
    share_h(2 * qyr, 2, rows1)
    arrived(b1_yfr)
    arrived(b1_yfl)
    share_h(2 * qyf, 2, rows1)
    arrived(b2_yf)
    share_h(2 * qyf, 2, rows2)

    step2_rest(0, 1 - yh, first0)
    step2_ready(1, yh)

    def dg_tile(m, _):
        rows = pl.ds(pl.multiple_of(m * 128, 128), 128)
        lhs = jnp.concatenate([h_all[s, rows, :] for s in range(16)], axis=1)
        dg[rows, :] = jnp.dot(lhs, g_all[c], preferred_element_type=F32).astype(BF16)
        return 0

    def down(first, last):
        lax.fori_loop(first, last, dg_tile, 0)

    for s in sib:
        arrived(s)
    arrived(c2y_f)
    bf = chip(xf, yh)
    add(p2.at[bf], (0, 256), [(r2y.at[xf], 0)])
    c2a_r = send(p2.at[bf, top], r2a.at[0], to_xr)
    c2a_l = send(p2.at[bf, low], r2a.at[1], to_xl)
    down(0, 4)
    step2_rest(1, yh, first1)
    down(4, 9)
    for s in c1[0]:
        arrived(s)
    bo = chip(x, 1 - yh)
    add(p1.at[bo], (0, 256), [(r1b.at[0, 0], 0), (r1b.at[1, 0], 0)])
    c1_y = send(p1.at[bo], r1y, to_yh)
    br, bl = chip(xr, yh), chip(xl, yh)
    arrived(c2y_r)
    add(p2.at[br], (128, 128), [(r2y.at[xr], 0)])
    c2_r = [send(p2.at[br, low], r2b.at[0, low], to_xr)]
    arrived(c2y_l)
    add(p2.at[bl], (0, 128), [(r2y.at[xl], 0)])
    c2_l = [send(p2.at[bl, top], r2b.at[1, top], to_xl)]
    down(9, 12)
    arrived(c2a_r)
    add(p2.at[br], (0, 128), [(r2y.at[xr], 0), (r2a.at[0], 0)])
    c2_r.append(send(p2.at[br, top], r2b.at[0, top], to_xr))
    arrived(c2a_l)
    add(p2.at[bl], (128, 128), [(r2y.at[xl], 0), (r2a.at[1], 128)])
    c2_l.append(send(p2.at[bl, low], r2b.at[1, low], to_xl))
    down(12, 26)

    own_rows = pl.multiple_of(c * 128, 128)
    sib_rows = pl.multiple_of((1 - c) * 128, 128)

    def total_of(first, dst, cols, terms):
        def strip(i, _):
            at = pl.ds(pl.multiple_of(first + i * 16, 16), 16)
            total = terms[0][at, :].astype(F32)
            for term in terms[1:]:
                total += term[at, :].astype(F32)
            dst[pl.ds(pl.multiple_of(i * 16, 16), 16), cols] = total
            return 0

        lax.fori_loop(0, 8, strip, 0)

    terms2 = [p2.at[q], r2y.at[x], r2b.at[0], r2b.at[1]]
    terms1 = [p1.at[q], r1b.at[0, 1], r1b.at[1, 1], r1y]
    cols1, cols2 = slice(0, N1), slice(N1, HALF)
    for s in c1[1]:
        arrived(s)
    arrived(c1_y)
    total_of(sib_rows, fin, cols1, terms1)
    last1 = send(fin.at[:, cols1], hg.at[c, :, cols1], to_core)
    total_of(own_rows, hg.at[c], cols1, terms1)
    for s in c2_r + c2_l + [c2y_o]:
        arrived(s)
    total_of(sib_rows, fin, cols2, terms2)
    last2 = send(fin.at[:, cols2], hg.at[c, :, cols2], to_core)
    total_of(own_rows, hg.at[c], cols2, terms2)
    arrived(last1)
    arrived(last2)
    net.finish()


BANDS = 13


def writer(dg, hg, gate, up, dg_out, gg_out, ug_out, buf, gg, ug, buf_sem, out_sem):
    rows = FFL // BANDS

    def band(k):
        slot = k % 4
        return pltpu.make_async_copy(buf.at[slot], dg_out.at[pl.ds(k * rows, rows)], buf_sem.at[slot])

    def finish(half):
        for k in range(HALF // 128):
            cols = slice(half * HALF + k * 128, half * HALF + (k + 1) * 128)
            grad = hg[half, :, k * 128 : (k + 1) * 128]
            gate_f = gate[:, cols].astype(F32)
            s = sigmoid(gate_f)
            gg[:, cols] = (grad * up[:, cols].astype(F32) * s * (1.0 + gate_f * (1.0 - s))).astype(BF16)
            ug[:, cols] = (grad * (gate_f * s)).astype(BF16)

    for k in range(BANDS):
        if k >= 4:
            band(k - 4).wait()
        buf[k % 4] = dg[k * rows : (k + 1) * rows, :].astype(F32)
        band(k).start()
        if k == 3:
            finish(0)
        if k == 7:
            finish(1)
            outs = [
                pltpu.make_async_copy(gg, gg_out, out_sem.at[0]),
                pltpu.make_async_copy(ug, ug_out, out_sem.at[1]),
            ]
            for out in outs:
                out.start()
    for k in range(BANDS - 4, BANDS):
        band(k).wait()
    for out in outs:
        out.wait()


def body(grad_values, row_scale, gate_input, up_input, down_weight):
    any_spec = pl.BlockSpec(memory_space=pl.ANY)
    vmem_spec = pl.BlockSpec(memory_space=pltpu.VMEM)
    held = pl.pallas_call(
        kernel,
        out_shape=(
            pltpu.VMEM((FFL, DL), BF16),
            pltpu.VMEM((2, 128, HALF), F32),
            pltpu.VMEM((128, FFL), BF16),
            pltpu.VMEM((128, FFL), BF16),
        ),
        in_specs=[any_spec, vmem_spec, any_spec, any_spec, any_spec],
        out_specs=(vmem_spec,) * 4,
        scratch_shapes=[
            pltpu.VMEM((2, TOK, DL), BF16),
            pltpu.VMEM((2, HALF, DL), BF16),
            pltpu.VMEM((16, FFL, 128), BF16),
            pltpu.VMEM((8, 256, N1), BF16),
            pltpu.VMEM((8, 256, N2), BF16),
            pltpu.VMEM((2, 2, 128, N1), BF16),
            pltpu.VMEM((2, 2, 256, N1), BF16),
            pltpu.VMEM((256, N1), BF16),
            pltpu.VMEM((4, 256, N2), BF16),
            pltpu.VMEM((2, 128, N2), BF16),
            pltpu.VMEM((2, 256, N2), BF16),
            pltpu.VMEM((128, HALF), F32),
            pltpu.VMEM((256, DL), BF16),
            pltpu.SemaphoreType.DMA((N_COPIES,)),
            pltpu.SemaphoreType.DMA((N_COPIES,)),
            pltpu.SemaphoreType.DMA((4,)),
        ],
        compiler_params=pltpu.CompilerParams(
            collective_id=0, has_side_effects=True, vmem_limit_bytes=48 * 2**20
        ),
        cost_estimate=pl.CostEstimate(flops=4 * TOK * FFL * DL, bytes_accessed=24 * 2**20, transcendentals=128 * FFL),
    )(grad_values, row_scale.reshape(2, 128), gate_input, up_input, down_weight)
    return pl.pallas_call(
        writer,
        out_shape=(
            jax.ShapeDtypeStruct((FFL, DL), F32),
            jax.ShapeDtypeStruct((128, FFL), BF16),
            jax.ShapeDtypeStruct((128, FFL), BF16),
        ),
        in_specs=[vmem_spec] * 4,
        out_specs=(any_spec,) * 3,
        scratch_shapes=[
            pltpu.VMEM((4, FFL // BANDS, DL), F32),
            pltpu.VMEM((128, FFL), BF16),
            pltpu.VMEM((128, FFL), BF16),
            pltpu.SemaphoreType.DMA((4,)),
            pltpu.SemaphoreType.DMA((2,)),
        ],
        compiler_params=pltpu.CompilerParams(vmem_limit_bytes=16 * 2**20),
        cost_estimate=pl.CostEstimate(flops=20 * 128 * FFL, bytes_accessed=24 * 2**20, transcendentals=128 * FFL),
    )(*held)


def solution(mesh):
    return jax.shard_map(
        body,
        mesh=mesh,
        in_specs=(
            P("tensor", "dp"),
            P("tensor"),
            P("dp", "tensor"),
            P("dp", "tensor"),
            P("tensor", "dp"),
        ),
        out_specs=(P("tensor", "dp"), P("dp", "tensor"), P("dp", "tensor")),
        check_vma=False,
    )
```

time: 150 us -> 115 us (0.77)
  Pallas kernels: 135 us -> 114 us
  local copies, waits for them, and re-layouts: 14.9 us -> 0 us
    pallas_call x1 -> x2, Pallas kernels: 135 us -> 114 us  [the longest x1 108 us: body(): pl.pallas_call(kernel, out_shape=(pltpu.VMEM((FFL, DL), BF16), pltpu.VMEM...]
    unnamed x7 -> x0, local copies, waits for them, and re-layouts: 14.9 us -> none
where the time goes in v2:
time: 115 us; the launch traced here: 114 us
  Pallas kernels  114 us (99%)
    pallas_call x1, Pallas kernels, body(): pl.pallas_call(kernel, out_shape=(pltpu.VMEM((FFL, DL), BF16), pltpu.VMEM...  108 us
    pallas_call x1, Pallas kernels, body(): pl.pallas_call(writer, out_shape=(jax.ShapeDtypeStruct((FFL, DL), F32), j...  5.56 us

profile of v2, /device:TPU:1, one launch (start us, length us, event | category | flops | bytes accessed | tf_op | source)
XLA Modules:
  0.0 114.4 jit_solution(14266133703365650137)
XLA Ops:
  0.6 108.2 %shard_map.76 = (bf16[3328,1024]{1,0:T(8,128)(2,1)S(1)}, f32[2,128,1664]{2,1,0:T(8,128)S(1)}, bf16[128,3328]{1,0:T(8,128)(2,1)S(1)}, bf16[128,3328]{1,0:T(8,128)(2,1)S(1)}) custom-call(bf16[256,1024]{1,0:T(8,128)(2,1)} %values.1, f32[2,128]{1,0:T(2,128)} %bitcast.1, bf16[128,3328]{1,0:T(8,128)(2,1)} %gate.1, bf16[128,3328]{1,0:T(8,128)(2,1)} %up.1, ...), custom_call_target="tpu_custom_call" | custom-call | flops 27917287424 | bytes 25165824 | tf_op jit(solution)/shard_map/pallas_call | solution.py:450
  108.9 5.6 %shard_map.77 = (f32[3328,1024]{1,0:T(8,128)}, bf16[128,3328]{1,0:T(8,128)(2,1)}, bf16[128,3328]{1,0:T(8,128)(2,1)}) custom-call(bf16[3328,1024]{1,0:T(8,128)(2,1)S(1)} %get-tuple-element.7.dg, f32[2,128,1664]{2,1,0:T(8,128)S(1)} %get-tuple-element.8.hg, bf16[128,3328]{1,0:T(8,128)(2,1)S(1)} %get-tuple-element.9.gate, bf16[128,3328]{1,0:T(8,128)(2,1)S(1)} %get-tuple-element.10.up), custom_call_target="tpu_custom_call" | custom-call | flops 8519680 | bytes 25165824 | tf_op jit(solution)/shard_map/pallas_call | solution.py:483

commit v3 on v2

--- a/solution.py
+++ b/solution.py
@@ -17,7 +17,9 @@
 DL = 1024
 N1 = 1024
 N2 = HALF - N1
-N_COPIES = 96
+B1 = 1024
+B2 = HALF - B1
+N_COPIES = 128
 
 
 def sigmoid(v):
@@ -123,7 +125,7 @@
     load_g.wait()
     load_u.wait()
 
-    def hidden(half):
+    def hidden(half, first, last):
         def tile(k, _):
             cols = pl.ds(pl.multiple_of(half * HALF + k * 128, 128), 128)
             gate_f = gate_in[:, cols].astype(F32)
@@ -131,25 +133,39 @@
             h_all[dp, cols, :] = h.T.astype(BF16)
             return 0
 
-        lax.fori_loop(0, HALF // 128, tile, 0, unroll=True)
-
-    base = pl.multiple_of(c * HALF, 128)
-    rows1 = pl.ds(base, N1)
-    rows2 = pl.ds(pl.multiple_of(base + N1, 128), N2)
+        lax.fori_loop(first, last, tile, 0, unroll=True)
+
+    def h_rows(half, first, count):
+        return pl.ds(pl.multiple_of(half * HALF + first, 16), count)
+
+    rows1 = h_rows(c, 0, B1)
+    rows1a, rows1b = h_rows(c, 0, B1 // 2), h_rows(c, B1 // 2, B1 // 2)
+    rows2 = h_rows(c, B1, B2)
 
     def send_h(first, count, rows, device):
         ref = h_all.at[pl.ds(first, count), rows]
         return send(ref, ref, device)
 
-    hidden(1 - c)
-    s_h = send_h(dp, 1, sib_half, to_core)
-    hidden(c)
-    arrived(s_h)
-    b2_xr = send_h(2 * q, 2, rows2, to_xr)
-    b2_xl = send_h(2 * q, 2, rows2, to_xl)
-    b1_y = send_h(2 * q, 2, rows1, to_yh)
-    b1_xr = send_h(2 * q, 2, rows1, to_xr)
-    b1_xl = send_h(2 * q, 2, rows1, to_xl)
+    twin = 2 * q + 1 - c
+    edge = B1 // 128
+    hidden(c, edge, HALF // 128)
+    b2_xr = [send_h(dp, 1, rows2, to_xr)]
+    b2_xl = [send_h(dp, 1, rows2, to_xl)]
+    hidden(1 - c, edge, HALF // 128)
+    s_h2 = send_h(dp, 1, h_rows(1 - c, B1, B2), to_core)
+    hidden(c, 0, edge)
+    b1_y = [send_h(dp, 1, rows1, to_yh)]
+    b1_xr = [send_h(dp, 1, rows1, to_xr)]
+    b1_xl = [send_h(dp, 1, rows1, to_xl)]
+    hidden(1 - c, 0, edge)
+    s_h1 = send_h(dp, 1, h_rows(1 - c, 0, B1), to_core)
+    arrived(s_h2)
+    b2_xr.append(send_h(twin, 1, rows2, to_xr))
+    b2_xl.append(send_h(twin, 1, rows2, to_xl))
+    arrived(s_h1)
+    b1_y.append(send_h(twin, 1, rows1, to_yh))
+    b1_xr.append(send_h(twin, 1, rows1, to_xr))
+    b1_xl.append(send_h(twin, 1, rows1, to_xl))
     b2_y = send_h(2 * q, 2, rows2, to_yh)
     load_w = load(3, weight.at[own_half], w_both.at[c])
     w_sib = send(weight.at[sib_half], w_both.at[c], to_core)
@@ -172,12 +188,8 @@
             )
             return total.astype(BF16)
 
-        def tile(n, _):
-            first = pl.multiple_of(n * 256, 256)
-            p1[block, :, pl.ds(first, 256)] = cols_of(first, 256)
-            return 0
-
-        lax.fori_loop(0, N1 // 256, tile, 0)
+        for first in range(0, N1, 512):
+            p1[block, :, first : first + 512] = cols_of(first, 512)
         p2[block, :, :] = cols_of(N1, N2)
 
     ql, qr, qf = chip(xl, yh), chip(xr, yh), chip(xf, yh)
@@ -185,11 +197,13 @@
     other = (1 - yl) * 4 + z
     ol, orr = (1 - yl) * 4 + zl, (1 - yl) * 4 + zr
 
-    arrived(b2_xr)
-    b2_fr = send_h(2 * ql, 1, rows2, to_xr)
+    for s in b2_xr:
+        arrived(s)
+    b2_fr = send_h(2 * ql + c, 1, rows2, to_xr)
     b2_yl = send_h(2 * ql, 2, rows2, to_yh)
-    arrived(b2_xl)
-    b2_fl = send_h(2 * qr + 1, 1, rows2, to_xl)
+    for s in b2_xl:
+        arrived(s)
+    b2_fl = send_h(2 * qr + 1 - c, 1, rows2, to_xl)
     b2_yr = send_h(2 * qr, 2, rows2, to_yh)
 
     arrived(a_yl)
@@ -216,10 +230,12 @@
 
     lax.fori_loop(0, 2, near, 0)
 
-    arrived(b1_xr)
-    b1_fr = send_h(2 * ql, 1, rows1, to_xr)
-    arrived(b1_xl)
-    b1_fl = send_h(2 * qr + 1, 1, rows1, to_xl)
+    for s in b1_xr:
+        arrived(s)
+    b1_fr = [send_h(2 * ql + c, 1, rows1a, to_xr)]
+    for s in b1_xl:
+        arrived(s)
+    b1_fl = [send_h(2 * qr + 1 - c, 1, rows1a, to_xl)]
 
     arrived(a_yzr)
     a_yfr = send_g(ol, to_zr, 0, 128)
@@ -228,9 +244,12 @@
     a_yfl = send_g(orr, to_zl, 128, 128)
     s_or = send_g(orr, to_core)
 
-    arrived(b1_y)
+    for s in b1_y:
+        arrived(s)
     b1_yxr = send_h(2 * qy, 2, rows1, to_xr)
     b1_yxl = send_h(2 * qy, 2, rows1, to_xl)
+    b1_fr.append(send_h(2 * ql + c, 1, rows1b, to_xr))
+    b1_fl.append(send_h(2 * qr + 1 - c, 1, rows1b, to_xl))
     share_h(2 * ql, 2, rows1)
     share_h(2 * qr, 2, rows1)
     share_h(2 * qy, 2, rows1)
@@ -311,8 +330,8 @@
     first1 = step1(1, yh)
     c2y_o = send(p2.at[chip(x, 1 - yh)], r2y.at[x], to_yh)
 
-    arrived(b1_fr)
-    arrived(b1_fl)
+    for s in b1_fr + b1_fl:
+        arrived(s)
     share_h(2 * qf, 2, rows1)
     arrived(b2_y)
     share_h(2 * qy, 2, rows2)
@@ -332,7 +351,7 @@
     step2_ready(1, yh)
 
     def dg_tile(m, _):
-        rows = pl.ds(pl.multiple_of(m * 128, 128), 128)
+        rows = pl.ds(pl.multiple_of(m * 256, 256), 256)
         lhs = jnp.concatenate([h_all[s, rows, :] for s in range(16)], axis=1)
         dg[rows, :] = jnp.dot(lhs, g_all[c], preferred_element_type=F32).astype(BF16)
         return 0
@@ -347,32 +366,35 @@
     add(p2.at[bf], (0, 256), [(r2y.at[xf], 0)])
     c2a_r = send(p2.at[bf, top], r2a.at[0], to_xr)
     c2a_l = send(p2.at[bf, low], r2a.at[1], to_xl)
-    down(0, 4)
+    down(0, 2)
     step2_rest(1, yh, first1)
-    down(4, 9)
+    down(2, 5)
     for s in c1[0]:
         arrived(s)
+    own_rows = pl.multiple_of(c * 128, 128)
+    sib_rows = pl.multiple_of((1 - c) * 128, 128)
     bo = chip(x, 1 - yh)
-    add(p1.at[bo], (0, 256), [(r1b.at[0, 0], 0), (r1b.at[1, 0], 0)])
-    c1_y = send(p1.at[bo], r1y, to_yh)
+    add(p1.at[bo], (sib_rows, 128), [(r1b.at[0, 0], 0), (r1b.at[1, 0], 0)])
+    c1_ys = send(p1.at[bo, pl.ds(sib_rows, 128)], r1y.at[pl.ds(sib_rows, 128)], to_yh)
+    add(p1.at[bo], (own_rows, 128), [(r1b.at[0, 0], 0), (r1b.at[1, 0], 0)])
+    c1_yo = send(p1.at[bo, pl.ds(own_rows, 128)], r1y.at[pl.ds(own_rows, 128)], to_yh)
     br, bl = chip(xr, yh), chip(xl, yh)
     arrived(c2y_r)
     add(p2.at[br], (128, 128), [(r2y.at[xr], 0)])
     c2_r = [send(p2.at[br, low], r2b.at[0, low], to_xr)]
+    down(5, 8)
     arrived(c2y_l)
     add(p2.at[bl], (0, 128), [(r2y.at[xl], 0)])
     c2_l = [send(p2.at[bl, top], r2b.at[1, top], to_xl)]
-    down(9, 12)
+    down(8, 10)
     arrived(c2a_r)
     add(p2.at[br], (0, 128), [(r2y.at[xr], 0), (r2a.at[0], 0)])
     c2_r.append(send(p2.at[br, top], r2b.at[0, top], to_xr))
     arrived(c2a_l)
     add(p2.at[bl], (128, 128), [(r2y.at[xl], 0), (r2a.at[1], 128)])
     c2_l.append(send(p2.at[bl, low], r2b.at[1, low], to_xl))
-    down(12, 26)
-
-    own_rows = pl.multiple_of(c * 128, 128)
-    sib_rows = pl.multiple_of((1 - c) * 128, 128)
+    down(10, 13)
+
 
     def total_of(first, dst, cols, terms):
         def strip(i, _):
@@ -388,17 +410,18 @@
     terms2 = [p2.at[q], r2y.at[x], r2b.at[0], r2b.at[1]]
     terms1 = [p1.at[q], r1b.at[0, 1], r1b.at[1, 1], r1y]
     cols1, cols2 = slice(0, N1), slice(N1, HALF)
-    for s in c1[1]:
-        arrived(s)
-    arrived(c1_y)
+    for s in c1[1] + [c2y_o]:
+        arrived(s)
+    arrived(c1_ys)
     total_of(sib_rows, fin, cols1, terms1)
     last1 = send(fin.at[:, cols1], hg.at[c, :, cols1], to_core)
-    total_of(own_rows, hg.at[c], cols1, terms1)
-    for s in c2_r + c2_l + [c2y_o]:
+    for s in c2_r + c2_l:
         arrived(s)
     total_of(sib_rows, fin, cols2, terms2)
     last2 = send(fin.at[:, cols2], hg.at[c, :, cols2], to_core)
     total_of(own_rows, hg.at[c], cols2, terms2)
+    arrived(c1_yo)
+    total_of(own_rows, hg.at[c], cols1, terms1)
     arrived(last1)
     arrived(last2)
     net.finish()

time: 115 us -> 111 us (0.965)
  Pallas kernels: 114 us -> 110 us
    pallas_call x1, Pallas kernels: 108 us -> 105 us  [body(): pl.pallas_call(kernel, out_shape=(pltpu.VMEM((FFL, DL), BF16), pltpu.VMEM...]
where the time goes in v3:
time: 111 us
  Pallas kernels  110 us (99%)
    pallas_call x1, Pallas kernels, body(): pl.pallas_call(kernel, out_shape=(pltpu.VMEM((FFL, DL), BF16), pltpu.VMEM...  105 us
    pallas_call x1, Pallas kernels, body(): pl.pallas_call(writer, out_shape=(jax.ShapeDtypeStruct((FFL, DL), F32), j...  5.56 us

profile of v3, /device:TPU:1, one launch (start us, length us, event | category | flops | bytes accessed | tf_op | source)
XLA Modules:
  0.0 110.8 jit_solution(11413039214823952111)
XLA Ops:
  0.6 104.6 %shard_map.76 = (bf16[3328,1024]{1,0:T(8,128)(2,1)S(1)}, f32[2,128,1664]{2,1,0:T(8,128)S(1)}, bf16[128,3328]{1,0:T(8,128)(2,1)S(1)}, bf16[128,3328]{1,0:T(8,128)(2,1)S(1)}) custom-call(bf16[256,1024]{1,0:T(8,128)(2,1)} %values.1, f32[2,128]{1,0:T(2,128)} %bitcast.1, bf16[128,3328]{1,0:T(8,128)(2,1)} %gate.1, bf16[128,3328]{1,0:T(8,128)(2,1)} %up.1, ...), custom_call_target="tpu_custom_call" | custom-call | flops 27917287424 | bytes 25165824 | tf_op jit(solution)/shard_map/pallas_call | solution.py:473
  105.2 5.6 %shard_map.77 = (f32[3328,1024]{1,0:T(8,128)}, bf16[128,3328]{1,0:T(8,128)(2,1)}, bf16[128,3328]{1,0:T(8,128)(2,1)}) custom-call(bf16[3328,1024]{1,0:T(8,128)(2,1)S(1)} %get-tuple-element.7.dg, f32[2,128,1664]{2,1,0:T(8,128)S(1)} %get-tuple-element.8.hg, bf16[128,3328]{1,0:T(8,128)(2,1)S(1)} %get-tuple-element.9.gate, bf16[128,3328]{1,0:T(8,128)(2,1)S(1)} %get-tuple-element.10.up), custom_call_target="tpu_custom_call" | custom-call | flops 8519680 | bytes 25165824 | tf_op jit(solution)/shard_map/pallas_call | solution.py:506

commit v4 on v3

--- a/solution.py
+++ b/solution.py
@@ -55,8 +55,8 @@
 
 def kernel(
     values, scale, gate, up, weight,
-    dg, hg, gate_in, up_in,
-    g_all, w_both, h_all, p1, p2, r1a, r1b, r1y, r2y, r2a, r2b, fin, v_in,
+    dg, s1, s2, gate_in, up_in,
+    g_all, w_both, h_all, p1, p2, r1a, r1b, r2y, r2a, v_in, scale_in,
     send_sem, recv_sem, load_sem,
 ):
     dp = lax.axis_index("dp")
@@ -76,6 +76,9 @@
     to_xr = (xr * 4 + yh * 2 + c, tensor)
     to_xl = (xl * 4 + yh * 2 + c, tensor)
     to_yh = (x * 4 + (1 - yh) * 2 + c, tensor)
+    to_xr_twin = (xr * 4 + yh * 2 + 1 - c, tensor)
+    to_xl_twin = (xl * 4 + yh * 2 + 1 - c, tensor)
+    to_yh_twin = (x * 4 + (1 - yh) * 2 + 1 - c, tensor)
     to_core = (q * 2 + (1 - c), tensor)
     to_yl = (dp, (1 - yl) * 4 + z)
     to_zr = (dp, yl * 4 + zr)
@@ -92,13 +95,16 @@
     own_half = pl.ds(pl.multiple_of(c * HALF, 128), HALF)
     sib_half = pl.ds(pl.multiple_of((1 - c) * HALF, 128), HALF)
     load_v = load(0, values, v_in)
+    load_s = load(4, scale, scale_in)
     load_g = load(1, gate, gate_in)
     load_u = load(2, up, up_in)
 
     barrier = pltpu.get_barrier_semaphore()
-    for neighbour in (to_xr, to_xl, to_yh, to_core, to_yl, to_zr, to_zl):
+    for neighbour in (
+        to_xr, to_xl, to_yh, to_core, to_yl, to_zr, to_zl, to_xr_twin, to_xl_twin, to_yh_twin
+    ):
         pl.semaphore_signal(barrier, inc=1, device_id=neighbour, device_id_type=MESH)
-    pl.semaphore_wait(barrier, 7)
+    pl.semaphore_wait(barrier, 10)
 
     net = Copies(send_sem, recv_sem)
     send, arrived = net.send, net.arrived
@@ -111,9 +117,10 @@
         return send(ref, ref, device)
 
     load_v.wait()
+    load_s.wait()
     own = tensor
     for i in range(2):
-        col = jnp.broadcast_to(scale[i : i + 1, :], (128, 128)).T
+        col = jnp.broadcast_to(scale_in[i : i + 1, :], (128, 128)).T
         for k in range(DL // 128):
             part = v_in[i * 128 : (i + 1) * 128, k * 128 : (k + 1) * 128].astype(F32) * col
             g_all[c, pl.ds(pl.multiple_of(own * 256 + i * 128, 128), 128), k * 128 : (k + 1) * 128] = part.astype(BF16)
@@ -289,19 +296,32 @@
 
     lax.fori_loop(0, 2, far, 0)
 
-    top, low = pl.ds(0, 128), pl.ds(128, 128)
+    own_at = pl.multiple_of(c * 128, 128)
+    sib_at = pl.multiple_of((1 - c) * 128, 128)
+    own_rows, sib_rows = pl.ds(own_at, 128), pl.ds(sib_at, 128)
     c1 = [[], []]
 
     def step1(place, yy):
         block = chip(xf, yy)
         return (
-            send(p1.at[block, top], r1a.at[0, place], to_xr),
-            send(p1.at[block, low], r1a.at[1, place], to_xl),
+            send(p1.at[block, own_rows], r1a.at[0, place], to_xr),
+            send(p1.at[block, sib_rows], r1a.at[1, place], to_xl),
         )
 
+    def step2(place, yy, own, right):
+        rows = own_rows if own else sib_rows
+        block = chip(xr if right else xl, yy)
+        if place == 0:
+            dst, device = r1b.at[0 if right else 1, rows], to_xr if right else to_xl
+        elif own:
+            dst, device = s1.at[1 if right else 2, c], to_xr if right else to_xl
+        else:
+            dst, device = s1.at[1 if right else 2, c], to_xr_twin if right else to_xl_twin
+        c1[place].append(send(p1.at[block, rows], dst, device))
+
     def step2_ready(place, yy):
-        c1[place].append(send(p1.at[chip(xr, yy), low], r1b.at[0, place, low], to_xr))
-        c1[place].append(send(p1.at[chip(xl, yy), top], r1b.at[1, place, top], to_xl))
+        step2(place, yy, False, True)
+        step2(place, yy, True, False)
 
     def add(dst, rows, others):
         def strip(i, _):
@@ -316,11 +336,11 @@
 
     def step2_rest(place, yy, first):
         arrived(first[0])
-        add(p1.at[chip(xr, yy)], (0, 128), [(r1a.at[0, place], 0)])
-        c1[place].append(send(p1.at[chip(xr, yy), top], r1b.at[0, place, top], to_xr))
+        add(p1.at[chip(xr, yy)], (own_at, 128), [(r1a.at[0, place], own_at)])
+        step2(place, yy, True, True)
         arrived(first[1])
-        add(p1.at[chip(xl, yy)], (128, 128), [(r1a.at[1, place], 128)])
-        c1[place].append(send(p1.at[chip(xl, yy), low], r1b.at[1, place, low], to_xl))
+        add(p1.at[chip(xl, yy)], (sib_at, 128), [(r1a.at[1, place], sib_at)])
+        step2(place, yy, False, False)
 
     first0 = step1(0, 1 - yh)
     c2y_f = send(p2.at[chip(xf, 1 - yh)], r2y.at[xf], to_yh)
@@ -329,6 +349,8 @@
     c2y_l = send(p2.at[chip(xl, 1 - yh)], r2y.at[xl], to_yh)
     first1 = step1(1, yh)
     c2y_o = send(p2.at[chip(x, 1 - yh)], r2y.at[x], to_yh)
+    keep1 = load(5, p1.at[q, own_rows], s1.at[0, c])
+    c1_core = send(p1.at[q, sib_rows], s1.at[0, c], to_core)
 
     for s in b1_fr + b1_fl:
         arrived(s)
@@ -364,104 +386,88 @@
     arrived(c2y_f)
     bf = chip(xf, yh)
     add(p2.at[bf], (0, 256), [(r2y.at[xf], 0)])
-    c2a_r = send(p2.at[bf, top], r2a.at[0], to_xr)
-    c2a_l = send(p2.at[bf, low], r2a.at[1], to_xl)
+    c2a_r = send(p2.at[bf, own_rows], r2a.at[0], to_xr)
+    c2a_l = send(p2.at[bf, sib_rows], r2a.at[1], to_xl)
     down(0, 2)
     step2_rest(1, yh, first1)
     down(2, 5)
     for s in c1[0]:
         arrived(s)
-    own_rows = pl.multiple_of(c * 128, 128)
-    sib_rows = pl.multiple_of((1 - c) * 128, 128)
     bo = chip(x, 1 - yh)
-    add(p1.at[bo], (sib_rows, 128), [(r1b.at[0, 0], 0), (r1b.at[1, 0], 0)])
-    c1_ys = send(p1.at[bo, pl.ds(sib_rows, 128)], r1y.at[pl.ds(sib_rows, 128)], to_yh)
-    add(p1.at[bo], (own_rows, 128), [(r1b.at[0, 0], 0), (r1b.at[1, 0], 0)])
-    c1_yo = send(p1.at[bo, pl.ds(own_rows, 128)], r1y.at[pl.ds(own_rows, 128)], to_yh)
+    add(p1.at[bo], (sib_at, 128), [(r1b.at[0], 0), (r1b.at[1], 0)])
+    c1_ys = send(p1.at[bo, sib_rows], s1.at[3, c], to_yh_twin)
+    add(p1.at[bo], (own_at, 128), [(r1b.at[0], 0), (r1b.at[1], 0)])
+    c1_yo = send(p1.at[bo, own_rows], s1.at[3, c], to_yh)
     br, bl = chip(xr, yh), chip(xl, yh)
     arrived(c2y_r)
-    add(p2.at[br], (128, 128), [(r2y.at[xr], 0)])
-    c2_r = [send(p2.at[br, low], r2b.at[0, low], to_xr)]
+    add(p2.at[br], (sib_at, 128), [(r2y.at[xr], 0)])
+    c2 = [send(p2.at[br, sib_rows], s2.at[1, c], to_xr_twin)]
     down(5, 8)
     arrived(c2y_l)
-    add(p2.at[bl], (0, 128), [(r2y.at[xl], 0)])
-    c2_l = [send(p2.at[bl, top], r2b.at[1, top], to_xl)]
+    add(p2.at[bl], (own_at, 128), [(r2y.at[xl], 0)])
+    c2.append(send(p2.at[bl, own_rows], s2.at[2, c], to_xl))
     down(8, 10)
     arrived(c2a_r)
-    add(p2.at[br], (0, 128), [(r2y.at[xr], 0), (r2a.at[0], 0)])
-    c2_r.append(send(p2.at[br, top], r2b.at[0, top], to_xr))
+    add(p2.at[br], (own_at, 128), [(r2y.at[xr], 0), (r2a.at[0], own_at)])
+    c2.append(send(p2.at[br, own_rows], s2.at[1, c], to_xr))
     arrived(c2a_l)
-    add(p2.at[bl], (128, 128), [(r2y.at[xl], 0), (r2a.at[1], 128)])
-    c2_l.append(send(p2.at[bl, low], r2b.at[1, low], to_xl))
+    add(p2.at[bl], (sib_at, 128), [(r2y.at[xl], 0), (r2a.at[1], sib_at)])
+    c2.append(send(p2.at[bl, sib_rows], s2.at[2, c], to_xl_twin))
+    arrived(c2y_o)
+    add(p2.at[q], (0, 256), [(r2y.at[x], 0)])
+    keep2 = load(6, p2.at[q, own_rows], s2.at[0, c])
+    c2_core = send(p2.at[q, sib_rows], s2.at[0, c], to_core)
     down(10, 13)
 
-
-    def total_of(first, dst, cols, terms):
-        def strip(i, _):
-            at = pl.ds(pl.multiple_of(first + i * 16, 16), 16)
-            total = terms[0][at, :].astype(F32)
-            for term in terms[1:]:
-                total += term[at, :].astype(F32)
-            dst[pl.ds(pl.multiple_of(i * 16, 16), 16), cols] = total
-            return 0
-
-        lax.fori_loop(0, 8, strip, 0)
-
-    terms2 = [p2.at[q], r2y.at[x], r2b.at[0], r2b.at[1]]
-    terms1 = [p1.at[q], r1b.at[0, 1], r1b.at[1, 1], r1y]
-    cols1, cols2 = slice(0, N1), slice(N1, HALF)
-    for s in c1[1] + [c2y_o]:
-        arrived(s)
-    arrived(c1_ys)
-    total_of(sib_rows, fin, cols1, terms1)
-    last1 = send(fin.at[:, cols1], hg.at[c, :, cols1], to_core)
-    for s in c2_r + c2_l:
-        arrived(s)
-    total_of(sib_rows, fin, cols2, terms2)
-    last2 = send(fin.at[:, cols2], hg.at[c, :, cols2], to_core)
-    total_of(own_rows, hg.at[c], cols2, terms2)
-    arrived(c1_yo)
-    total_of(own_rows, hg.at[c], cols1, terms1)
-    arrived(last1)
-    arrived(last2)
+    keep1.wait()
+    keep2.wait()
+    for s in [c1_core, c2_core, c1_ys, c1_yo] + c1[1] + c2:
+        arrived(s)
     net.finish()
 
 
 BANDS = 13
-
-
-def writer(dg, hg, gate, up, dg_out, gg_out, ug_out, buf, gg, ug, buf_sem, out_sem):
+SLOTS = 6
+
+
+def writer(dg, s1, s2, gate, up, dg_out, gg_out, ug_out, buf, gg, ug, buf_sem, out_sem):
     rows = FFL // BANDS
 
     def band(k):
-        slot = k % 4
+        slot = k % SLOTS
         return pltpu.make_async_copy(buf.at[slot], dg_out.at[pl.ds(k * rows, rows)], buf_sem.at[slot])
 
-    def finish(half):
-        for k in range(HALF // 128):
-            cols = slice(half * HALF + k * 128, half * HALF + (k + 1) * 128)
-            grad = hg[half, :, k * 128 : (k + 1) * 128]
-            gate_f = gate[:, cols].astype(F32)
-            s = sigmoid(gate_f)
-            gg[:, cols] = (grad * up[:, cols].astype(F32) * s * (1.0 + gate_f * (1.0 - s))).astype(BF16)
-            ug[:, cols] = (grad * (gate_f * s)).astype(BF16)
-
+    def finish(half, k):
+        cols = slice(half * HALF + k * 128, half * HALF + (k + 1) * 128)
+        first, terms = k * 128, s1
+        if first >= N1:
+            first, terms = first - N1, s2
+        grad = terms[0, half, :, first : first + 128].astype(F32)
+        for i in range(1, terms.shape[0]):
+            grad += terms[i, half, :, first : first + 128].astype(F32)
+        gate_f = gate[:, cols].astype(F32)
+        s = sigmoid(gate_f)
+        gg[:, cols] = (grad * up[:, cols].astype(F32) * s * (1.0 + gate_f * (1.0 - s))).astype(BF16)
+        ug[:, cols] = (grad * (gate_f * s)).astype(BF16)
+
+    tiles = [(half, k) for half in range(2) for k in range(HALF // 128)]
+    outs = []
     for k in range(BANDS):
-        if k >= 4:
-            band(k - 4).wait()
-        buf[k % 4] = dg[k * rows : (k + 1) * rows, :].astype(F32)
+        if k >= SLOTS:
+            for tile in tiles[:5]:
+                finish(*tile)
+            del tiles[:5]
+            if not tiles and not outs:
+                outs = [
+                    pltpu.make_async_copy(gg, gg_out, out_sem.at[0]),
+                    pltpu.make_async_copy(ug, ug_out, out_sem.at[1]),
+                ]
+                for out in outs:
+                    out.start()
+            band(k - SLOTS).wait()
+        buf[k % SLOTS] = dg[k * rows : (k + 1) * rows, :].astype(F32)
         band(k).start()
-        if k == 3:
-            finish(0)
-        if k == 7:
-            finish(1)
-            outs = [
-                pltpu.make_async_copy(gg, gg_out, out_sem.at[0]),
-                pltpu.make_async_copy(ug, ug_out, out_sem.at[1]),
-            ]
-            for out in outs:
-                out.start()
-    for k in range(BANDS - 4, BANDS):
+    for k in range(BANDS - SLOTS, BANDS):
         band(k).wait()
     for out in outs:
         out.wait()
@@ -474,12 +480,13 @@
         kernel,
         out_shape=(
             pltpu.VMEM((FFL, DL), BF16),
-            pltpu.VMEM((2, 128, HALF), F32),
+            pltpu.VMEM((4, 2, 128, N1), BF16),
+            pltpu.VMEM((3, 2, 128, N2), BF16),
             pltpu.VMEM((128, FFL), BF16),
             pltpu.VMEM((128, FFL), BF16),
         ),
-        in_specs=[any_spec, vmem_spec, any_spec, any_spec, any_spec],
-        out_specs=(vmem_spec,) * 4,
+        in_specs=[any_spec] * 5,
+        out_specs=(vmem_spec,) * 5,
         scratch_shapes=[
             pltpu.VMEM((2, TOK, DL), BF16),
             pltpu.VMEM((2, HALF, DL), BF16),
@@ -487,19 +494,17 @@
             pltpu.VMEM((8, 256, N1), BF16),
             pltpu.VMEM((8, 256, N2), BF16),
             pltpu.VMEM((2, 2, 128, N1), BF16),
-            pltpu.VMEM((2, 2, 256, N1), BF16),
-            pltpu.VMEM((256, N1), BF16),
+            pltpu.VMEM((2, 256, N1), BF16),
             pltpu.VMEM((4, 256, N2), BF16),
             pltpu.VMEM((2, 128, N2), BF16),
-            pltpu.VMEM((2, 256, N2), BF16),
-            pltpu.VMEM((128, HALF), F32),
             pltpu.VMEM((256, DL), BF16),
+            pltpu.VMEM((2, 128), F32),
             pltpu.SemaphoreType.DMA((N_COPIES,)),
             pltpu.SemaphoreType.DMA((N_COPIES,)),
-            pltpu.SemaphoreType.DMA((4,)),
+            pltpu.SemaphoreType.DMA((7,)),
         ],
         compiler_params=pltpu.CompilerParams(
-            collective_id=0, has_side_effects=True, vmem_limit_bytes=48 * 2**20
+            collective_id=0, has_side_effects=True, vmem_limit_bytes=46 * 2**20
         ),
         cost_estimate=pl.CostEstimate(flops=4 * TOK * FFL * DL, bytes_accessed=24 * 2**20, transcendentals=128 * FFL),
     )(grad_values, row_scale.reshape(2, 128), gate_input, up_input, down_weight)
@@ -510,16 +515,16 @@
             jax.ShapeDtypeStruct((128, FFL), BF16),
             jax.ShapeDtypeStruct((128, FFL), BF16),
         ),
-        in_specs=[vmem_spec] * 4,
+        in_specs=[vmem_spec] * 5,
         out_specs=(any_spec,) * 3,
         scratch_shapes=[
-            pltpu.VMEM((4, FFL // BANDS, DL), F32),
+            pltpu.VMEM((SLOTS, FFL // BANDS, DL), F32),
             pltpu.VMEM((128, FFL), BF16),
             pltpu.VMEM((128, FFL), BF16),
-            pltpu.SemaphoreType.DMA((4,)),
+            pltpu.SemaphoreType.DMA((SLOTS,)),
             pltpu.SemaphoreType.DMA((2,)),
         ],
-        compiler_params=pltpu.CompilerParams(vmem_limit_bytes=16 * 2**20),
+        compiler_params=pltpu.CompilerParams(vmem_limit_bytes=20 * 2**20),
         cost_estimate=pl.CostEstimate(flops=20 * 128 * FFL, bytes_accessed=24 * 2**20, transcendentals=128 * FFL),
     )(*held)
 

time: 111 us -> 110 us (level)
    pallas_call x1, Pallas kernels: 105 us -> 103 us  [body(): pl.pallas_call(kernel, out_shape=(pltpu.VMEM((FFL, DL), BF16), pltpu.VMEM...]
where the time goes in v4:
time: 110 us; the launch traced here: 109 us
  Pallas kernels  109 us (99%)
    pallas_call x1, Pallas kernels, body(): pl.pallas_call(kernel, out_shape=(pltpu.VMEM((FFL, DL), BF16), pltpu.VMEM...  103 us
    pallas_call x1, Pallas kernels, body(): pl.pallas_call(writer, out_shape=(jax.ShapeDtypeStruct((FFL, DL), F32), j...  5.53 us

profile of v4, /device:TPU:1, one launch (start us, length us, event | category | flops | bytes accessed | tf_op | source)
XLA Modules:
  0.0 109.4 jit_solution(9325758389019206269)
XLA Ops:
  0.6 103.1 %shard_map.76 = (bf16[3328,1024]{1,0:T(8,128)(2,1)S(1)}, bf16[4,2,128,1024]{3,2,1,0:T(8,128)(2,1)S(1)}, bf16[3,2,128,640]{3,2,1,0:T(8,128)(2,1)S(1)}, bf16[128,3328]{1,0:T(8,128)(2,1)S(1)}, bf16[128,3328]{1,0:T(8,128)(2,1)S(1)}) custom-call(bf16[256,1024]{1,0:T(8,128)(2,1)} %values.1, f32[2,128]{1,0:T(2,128)} %bitcast.1, bf16[128,3328]{1,0:T(8,128)(2,1)} %gate.1, ...), custom_call_target="tpu_custom_call" | custom-call | flops 27917287424 | bytes 25165824 | tf_op jit(solution)/shard_map/pallas_call | solution.py:479
  103.8 5.5 %shard_map.77 = (f32[3328,1024]{1,0:T(8,128)}, bf16[128,3328]{1,0:T(8,128)(2,1)}, bf16[128,3328]{1,0:T(8,128)(2,1)}) custom-call(bf16[3328,1024]{1,0:T(8,128)(2,1)S(1)} %get-tuple-element.8.dg, bf16[4,2,128,1024]{3,2,1,0:T(8,128)(2,1)S(1)} %get-tuple-element.9.s1, bf16[3,2,128,640]{3,2,1,0:T(8,128)(2,1)S(1)} %get-tuple-element.10.s2, ...), custom_call_target="tpu_custom_call" | custom-call | flops 8519680 | bytes 25165824 | tf_op jit(solution)/shard_map/pallas_call | solution.py:511

commit v5 on v4

--- a/solution.py
+++ b/solution.py
@@ -124,7 +124,7 @@
         for k in range(DL // 128):
             part = v_in[i * 128 : (i + 1) * 128, k * 128 : (k + 1) * 128].astype(F32) * col
             g_all[c, pl.ds(pl.multiple_of(own * 256 + i * 128, 128), 128), k * 128 : (k + 1) * 128] = part.astype(BF16)
-    a_yl = send_g(own, to_yl)
+    a_yl = [send_g(own, to_yl, first, 128) for first in (0, 128)]
     a_zr = send_g(own, to_zr)
     a_zl = send_g(own, to_zl)
     s_own = send_g(own, to_core)
@@ -204,18 +204,11 @@
     other = (1 - yl) * 4 + z
     ol, orr = (1 - yl) * 4 + zl, (1 - yl) * 4 + zr
 
-    for s in b2_xr:
-        arrived(s)
-    b2_fr = send_h(2 * ql + c, 1, rows2, to_xr)
-    b2_yl = send_h(2 * ql, 2, rows2, to_yh)
-    for s in b2_xl:
-        arrived(s)
-    b2_fl = send_h(2 * qr + 1 - c, 1, rows2, to_xl)
-    b2_yr = send_h(2 * qr, 2, rows2, to_yh)
-
-    arrived(a_yl)
-    a_yzr = send_g(other, to_zr)
-    a_yzl = send_g(other, to_zl)
+    a_yzr, a_yzl = [], []
+    for first, s in zip((0, 128), a_yl):
+        arrived(s)
+        a_yzr.append(send_g(other, to_zr, first, 128))
+        a_yzl.append(send_g(other, to_zl, first, 128))
     s_other = send_g(other, to_core)
     arrived(a_zr)
     a_fr = send_g(yl * 4 + zl, to_zr, 0, 128)
@@ -223,6 +216,15 @@
     arrived(a_zl)
     a_fl = send_g(yl * 4 + zr, to_zl, 128, 128)
     s_zr = send_g(yl * 4 + zr, to_core)
+    for s in b2_xr:
+        arrived(s)
+    b2_fr = send_h(2 * ql + c, 1, rows2, to_xr)
+    b2_yl = send_h(2 * ql, 2, rows2, to_yh)
+    for s in b2_xl:
+        arrived(s)
+    b2_fl = send_h(2 * qr + 1 - c, 1, rows2, to_xl)
+    b2_yr = send_h(2 * qr, 2, rows2, to_yh)
+
     share_h(2 * ql, 2, rows2)
     share_h(2 * qr, 2, rows2)
 
@@ -244,10 +246,12 @@
         arrived(s)
     b1_fl = [send_h(2 * qr + 1 - c, 1, rows1a, to_xl)]
 
-    arrived(a_yzr)
+    for s in a_yzr:
+        arrived(s)
     a_yfr = send_g(ol, to_zr, 0, 128)
     s_ol = send_g(ol, to_core)
-    arrived(a_yzl)
+    for s in a_yzl:
+        arrived(s)
     a_yfl = send_g(orr, to_zl, 128, 128)
     s_or = send_g(orr, to_core)
 

time: 110 us -> 107 us (0.973)
  Pallas kernels: 109 us -> 106 us
    pallas_call x1, Pallas kernels: 103 us -> 101 us  [body(): pl.pallas_call(kernel, out_shape=(pltpu.VMEM((FFL, DL), BF16), pltpu.VMEM...]
where the time goes in v5:
time: 107 us
  Pallas kernels  106 us (99%)
    pallas_call x1, Pallas kernels, body(): pl.pallas_call(kernel, out_shape=(pltpu.VMEM((FFL, DL), BF16), pltpu.VMEM...  101 us
    pallas_call x1, Pallas kernels, body(): pl.pallas_call(writer, out_shape=(jax.ShapeDtypeStruct((FFL, DL), F32), j...  5.53 us

profile of v5, /device:TPU:1, one launch (start us, length us, event | category | flops | bytes accessed | tf_op | source)
XLA Modules:
  0.0 106.9 jit_solution(1949750344613554308)
XLA Ops:
  0.6 100.6 %shard_map.76 = (bf16[3328,1024]{1,0:T(8,128)(2,1)S(1)}, bf16[4,2,128,1024]{3,2,1,0:T(8,128)(2,1)S(1)}, bf16[3,2,128,640]{3,2,1,0:T(8,128)(2,1)S(1)}, bf16[128,3328]{1,0:T(8,128)(2,1)S(1)}, bf16[128,3328]{1,0:T(8,128)(2,1)S(1)}) custom-call(bf16[256,1024]{1,0:T(8,128)(2,1)} %values.1, f32[2,128]{1,0:T(2,128)} %bitcast.1, bf16[128,3328]{1,0:T(8,128)(2,1)} %gate.1, ...), custom_call_target="tpu_custom_call" | custom-call | flops 27917287424 | bytes 25165824 | tf_op jit(solution)/shard_map/pallas_call | solution.py:483
  101.2 5.5 %shard_map.77 = (f32[3328,1024]{1,0:T(8,128)}, bf16[128,3328]{1,0:T(8,128)(2,1)}, bf16[128,3328]{1,0:T(8,128)(2,1)}) custom-call(bf16[3328,1024]{1,0:T(8,128)(2,1)S(1)} %get-tuple-element.8.dg, bf16[4,2,128,1024]{3,2,1,0:T(8,128)(2,1)S(1)} %get-tuple-element.9.s1, bf16[3,2,128,640]{3,2,1,0:T(8,128)(2,1)S(1)} %get-tuple-element.10.s2, ...), custom_call_target="tpu_custom_call" | custom-call | flops 8519680 | bytes 25165824 | tf_op jit(solution)/shard_map/pallas_call | solution.py:515

commit v6 on v5

--- a/solution.py
+++ b/solution.py
@@ -104,7 +104,6 @@
         to_xr, to_xl, to_yh, to_core, to_yl, to_zr, to_zl, to_xr_twin, to_xl_twin, to_yh_twin
     ):
         pl.semaphore_signal(barrier, inc=1, device_id=neighbour, device_id_type=MESH)
-    pl.semaphore_wait(barrier, 10)
 
     net = Copies(send_sem, recv_sem)
     send, arrived = net.send, net.arrived
@@ -124,6 +123,7 @@
         for k in range(DL // 128):
             part = v_in[i * 128 : (i + 1) * 128, k * 128 : (k + 1) * 128].astype(F32) * col
             g_all[c, pl.ds(pl.multiple_of(own * 256 + i * 128, 128), 128), k * 128 : (k + 1) * 128] = part.astype(BF16)
+    pl.semaphore_wait(barrier, 10)
     a_yl = [send_g(own, to_yl, first, 128) for first in (0, 128)]
     a_zr = send_g(own, to_zr)
     a_zl = send_g(own, to_zl)
@@ -246,6 +246,17 @@
         arrived(s)
     b1_fl = [send_h(2 * qr + 1 - c, 1, rows1a, to_xl)]
 
+    def products(y_lo):
+        def middle(i, _):
+            product(y_lo * 4 + wrap(z - 1 + 2 * i))
+            return 0
+
+        lax.fori_loop(0, 2, middle, 0)
+
+    arrived(s_zl)
+    arrived(s_zr)
+    products(yl)
+
     for s in a_yzr:
         arrived(s)
     a_yfr = send_g(ol, to_zr, 0, 128)
@@ -270,14 +281,9 @@
     b2_yf = send_h(2 * qf, 2, rows2, to_yh)
     share_h(2 * qf, 2, rows2)
 
-    for s in (s_zl, s_zr, s_ol, s_or):
-        arrived(s)
-
-    def middle(i, _):
-        product((i // 2) * 4 + wrap(z - 1 + 2 * lax.rem(i, 2)))
-        return 0
-
-    lax.fori_loop(0, 4, middle, 0)
+    arrived(s_ol)
+    arrived(s_or)
+    products(1 - yl)
 
     arrived(a_fr)
     arrived(a_fl)

time: 107 us -> 107 us (level)
  no operation moved by 1% of the time
where the time goes in v6:
time: 107 us
  Pallas kernels  106 us (99%)
    pallas_call x1, Pallas kernels, body(): pl.pallas_call(kernel, out_shape=(pltpu.VMEM((FFL, DL), BF16), pltpu.VMEM...  100 us
    pallas_call x1, Pallas kernels, body(): pl.pallas_call(writer, out_shape=(jax.ShapeDtypeStruct((FFL, DL), F32), j...  5.53 us

profile of v6, /device:TPU:1, one launch (start us, length us, event | category | flops | bytes accessed | tf_op | source)
XLA Modules:
  0.0 106.7 jit_solution(683185417703969291)
XLA Ops:
  0.6 100.4 %shard_map.76 = (bf16[3328,1024]{1,0:T(8,128)(2,1)S(1)}, bf16[4,2,128,1024]{3,2,1,0:T(8,128)(2,1)S(1)}, bf16[3,2,128,640]{3,2,1,0:T(8,128)(2,1)S(1)}, bf16[128,3328]{1,0:T(8,128)(2,1)S(1)}, bf16[128,3328]{1,0:T(8,128)(2,1)S(1)}) custom-call(bf16[256,1024]{1,0:T(8,128)(2,1)} %values.1, f32[2,128]{1,0:T(2,128)} %bitcast.1, bf16[128,3328]{1,0:T(8,128)(2,1)} %gate.1, ...), custom_call_target="tpu_custom_call" | custom-call | flops 27917287424 | bytes 25165824 | tf_op jit(solution)/shard_map/pallas_call | solution.py:489
  101.0 5.5 %shard_map.77 = (f32[3328,1024]{1,0:T(8,128)}, bf16[128,3328]{1,0:T(8,128)(2,1)}, bf16[128,3328]{1,0:T(8,128)(2,1)}) custom-call(bf16[3328,1024]{1,0:T(8,128)(2,1)S(1)} %get-tuple-element.8.dg, bf16[4,2,128,1024]{3,2,1,0:T(8,128)(2,1)S(1)} %get-tuple-element.9.s1, bf16[3,2,128,640]{3,2,1,0:T(8,128)(2,1)S(1)} %get-tuple-element.10.s2, ...), custom_call_target="tpu_custom_call" | custom-call | flops 8519680 | bytes 25165824 | tf_op jit(solution)/shard_map/pallas_call | solution.py:521
